TPU v7x, 32 devices: a whole 2x2x4 slice. The times are simulated.
32 devices in a mesh: face: 4 (over y, core), tile: 8 (over z, x).
Axes of the slice: x: 2, y: 2, z: 4, core: 2. Of those that a mesh axis runs over, the one named last changes fastest.
Arguments:
- met_src: bfloat16 [2048, 48, 128], P(('face', 'tile')), may hold values from -6 to 6
- intersection_weights: bfloat16 [2048, 128, 128], P(('face', 'tile')), may hold values from -0.5 to 0.5
- block_dest: int32 [2048], P(('face', 'tile')), may hold values from 0 to 31, as said below
- block_row: int32 [2048], P(('face', 'tile')), may hold values from 0 to 15
- tracers: float32 [250, 4, 64, 1024], P(None, None, 'face', 'tile'), may hold values from 0.1 to 10
- rate_coef: float32 [250, 12], replicated, may hold values from -1.75 to 1.75
- photo_coef: float32 [250], replicated, may hold values from 0.1 to 3
Outputs:
- met_tile: float32 [12, 4, 64, 1024], P(None, None, 'face', 'tile')
- species_out: float32 [250, 4, 64, 1024], P(None, None, 'face', 'tile')
Inputs may be any that keep to these rules, and one draw needn't show every extreme that they name: `block_dest`: each source owner (the 64 blocks of one device) names any one tile owner at most 2 times; in every draw some tile owner is named exactly 2 times by every source owner.
All inputs are finite; a program needn't handle non-finite values.
Results may differ from a plain program's by a relative error of at most 0.0029.
Values may be sent and summed in bfloat16 or wider, within the bound.
No kernel may reach another device: no remote copies, remote signals or barrier semaphores. Data moves between devices by JAX's collectives and lax.ppermute only.
A program may use at most 128 MiB of HBM per device.

v0:
```python
import jax
import jax.numpy as jnp
from jax import lax
from jax.sharding import PartitionSpec as P

CAP = 2
ADV_STEPS = 2


def with_halo(block, sides, width):
    for axis, dim in sides:
        count = lax.axis_size(axis)
        forward = [(i, i + 1) for i in range(count - 1)]
        forward.append((count - 1, 0))
        backward = [(target, source) for source, target in forward]
        low = lax.ppermute(
            lax.slice_in_dim(block, block.shape[dim] - width, None, axis=dim), axis, forward
        )
        high = lax.ppermute(lax.slice_in_dim(block, 0, width, axis=dim), axis, backward)
        block = jnp.concatenate([low, block, high], axis=dim)
    return block


def deliver(packed, slot_label):
    arrived, labels = (
        lax.all_to_all(packed, ("face", "tile"), split_axis=0, concat_axis=0, tiled=True),
        lax.all_to_all(slot_label, ("face", "tile"), split_axis=0, concat_axis=0, tiled=True),
    )
    return (arrived, labels)


def local(met_src, intersection_weights, block_dest, block_row, tracers, rate_coef, photo_coef):
    n_face = lax.axis_size("face")
    n_tile = lax.axis_size("tile")
    owner_count = n_face * n_tile
    blocks, levfields, cell_count = met_src.shape
    nfields = rate_coef.shape[1]
    levels = levfields // nfields
    rows_x = tracers.shape[2]
    slot_count = owner_count * CAP
    owners = jnp.arange(owner_count, dtype=jnp.int32)
    matches = (block_dest[:, None] == owners[None, :]).astype(jnp.int32)
    earlier_count = jnp.cumsum(matches, axis=0) - 1
    own_rank = jnp.sum(earlier_count * matches, axis=1)
    position = block_dest * CAP + own_rank
    placer = (jnp.arange(slot_count, dtype=jnp.int32)[:, None] == position[None, :]).astype(
        jnp.bfloat16
    )
    slot_label = (
        jnp.dot(placer, (block_row + 1).astype(jnp.bfloat16), preferred_element_type=jnp.float32)
        - 1.0
    ).astype(jnp.bfloat16)
    contrib = jnp.einsum(
        "sfi,sij->sfj", met_src, intersection_weights, preferred_element_type=jnp.float32
    ).astype(jnp.bfloat16)
    payload = contrib.reshape(blocks, levfields * cell_count)
    packed = jnp.dot(placer, payload, preferred_element_type=jnp.float32).astype(jnp.bfloat16)
    arrived, labels = deliver(packed, slot_label)
    received = arrived.reshape(slot_count, levfields, cell_count)
    row_values = jnp.arange(rows_x).astype(jnp.bfloat16)
    chooser = (labels[:, None] == row_values[None, :]).astype(jnp.bfloat16)
    met_flat = jnp.einsum("rt,rfc->ftc", chooser, received, preferred_element_type=jnp.float32)
    met_tile = met_flat.reshape(nfields, levels, rows_x, cell_count)
    courant_x = 0.3 * jnp.tanh(met_tile[0])
    courant_y = 0.3 * jnp.tanh(met_tile[1])
    rim_depth = ADV_STEPS
    stacked = jnp.stack([courant_x, courant_y])
    wind_field = with_halo(stacked, (("face", 2), ("tile", 3)), rim_depth)
    amount = with_halo(tracers, (("face", 2), ("tile", 3)), rim_depth)
    for substep in range(ADV_STEPS):
        rows_now = rows_x + 2 * (rim_depth - substep)
        cols_now = cell_count + 2 * (rim_depth - substep)
        window = wind_field[:, :, substep : substep + rows_now, substep : substep + cols_now]
        wind_x = window[0]
        wind_y = window[1]
        flux_x = (
            jnp.maximum(wind_x[:, :-1, 1:-1], 0.0) * amount[:, :, :-1, 1:-1]
            + jnp.minimum(wind_x[:, :-1, 1:-1], 0.0) * amount[:, :, 1:, 1:-1]
        )
        flux_y = (
            jnp.maximum(wind_y[:, 1:-1, :-1], 0.0) * amount[:, :, 1:-1, :-1]
            + jnp.minimum(wind_y[:, 1:-1, :-1], 0.0) * amount[:, :, 1:-1, 1:]
        )
        amount = (
            amount[:, :, 1:-1, 1:-1]
            - (flux_x[:, :, 1:, :] - flux_x[:, :, :-1, :])
            - (flux_y[:, :, :, 1:] - flux_y[:, :, :, :-1])
        )
    column_depth = jnp.cumsum(jax.nn.softplus(met_tile[2]), axis=0)
    light = jnp.exp(-column_depth)
    exponent = (
        jnp.einsum("sf,flxy->slxy", rate_coef, met_tile, precision=lax.Precision.HIGHEST)
        + photo_coef[:, None, None, None] * light[None]
    )
    species_out = amount / (1.0 + jax.nn.softplus(exponent))
    return (met_tile, species_out)


def solution(mesh):
    return jax.shard_map(
        local,
        mesh=mesh,
        in_specs=(
            P(("face", "tile"), None, None),
            P(("face", "tile"), None, None),
            P(("face", "tile")),
            P(("face", "tile")),
            P(None, None, "face", "tile"),
            P(),
            P(),
        ),
        out_specs=(P(None, None, "face", "tile"), P(None, None, "face", "tile")),
        check_vma=False,
    )
```

profile of v0, /device:TPU:0, one launch (start us, length us, event | category | flops | bytes accessed | tf_op | source)
XLA Modules:
  0.0 164.7 jit_solution(12529170551914906668)
XLA Ops:
  0.6 0.9 fusion.29
  1.6 0.8 select_reduce_fusion
  3.1 0.8 fusion.12
  4.7 7.3 %all-to-all-start.1 = ((bf16[32,2,1]{1,2,0:T(2,128)(2,1)}), bf16[32,2,1]{1,2,0:T(2,128)(2,1)S(1)}, u32[]{:S(2)}, u32[]{:S(2)}) async-start(bf16[32,2,1]{1,2,0:T(2,128)(2,1)} %all_to_all.16), calls=%async_computation.1 | async-start | bytes 32768 | tf_op jit(solution)/shard_map/all_to_all | solution.py:27
  12.0 1.8 %convolution_convert_fusion.1 = bf16[64,48,128]{2,1,0:T(8,128)(2,1)S(1)} fusion(bf16[64,48,128]{2,1,0:T(8,128)(2,1)} %param.7, bf16[64,128,128]{2,1,0:T(8,128)(2,1)S(1)} %copy-done), kind=kOutput, calls=%fused_computation.26 | convolution fusion | flops 101056512 | bytes 3670016 | tf_op jit(solution)/shard_map/sfi,sij->sfj/dot_general | solution.py:53
  14.2 1.4 all_to_all.12
  15.6 3.4 %all-to-all-done.1 = bf16[32,2,1]{1,2,0:T(2,128)(2,1)S(1)} async-done(((bf16[32,2,1]{1,2,0:T(2,128)(2,1)}), bf16[32,2,1]{1,2,0:T(2,128)(2,1)S(1)}, u32[]{:S(2)}, u32[]{:S(2)}) %all-to-all-start.1) | async-done | bytes 160 | tf_op jit(solution)/shard_map/all_to_all | solution.py:27
  19.0 2.6 %all-to-all-start = ((bf16[32,2,6144]{2,1,0:T(2,128)(2,1)}), bf16[32,2,6144]{2,1,0:T(2,128)(2,1)S(1)}, u32[]{:S(2)}, u32[]{:S(2)}) async-start(bf16[32,2,6144]{2,1,0:T(2,128)(2,1)} %all_to_all.12), calls=%async_computation | async-start | bytes 1572864 | tf_op jit(solution)/shard_map/all_to_all | solution.py:26
  21.6 4.4 %fusion.42 = (f32[250,4,2,128]{3,2,1,0:T(2,128)S(1)}, f32[250,4,2,128]{3,2,1,0:T(2,128)S(1)}) fusion(f32[250,4,16,128]{3,2,1,0:T(8,128)} %param.11), kind=kLoop, calls=%fused_computation.89 | loop fusion | bytes 4096000 | tf_op jit(solution)/shard_map/slice | solution.py:17
  26.1 1.2 copy.30
  27.4 1.2 copy.31
  28.6 1.6 collective-permute-start.1
  30.3 10.0 %copy.25 = f32[250,4,16,128]{0,3,2,1:T(8,128)} copy(f32[250,4,16,128]{3,2,1,0:T(8,128)} %param.11) | data formatting | bytes 16384000 | tf_op args[4]
  40.4 14.3 %collective-permute-done = f32[250,4,2,128]{3,1,2,0:T(4,128)S(1)} collective-permute-done((f32[250,4,2,128]{3,1,2,0:T(4,128)}, f32[250,4,2,128]{3,1,2,0:T(4,128)S(1)}, u32[]{:S(2)}, u32[]{:S(2)}) %collective-permute-start) | collective-permute-done | bytes 1024032 | tf_op jit(solution)/shard_map/ppermute | solution.py:16
  55.3 1.6 copy.26
  56.8 1.3 pad_maximum_fusion.4
  58.2 1.6 collective-permute-start.2
  59.8 3.2 %collective-permute-start.3 = (f32[250,4,20,2]{0,3,2,1:T(2,128)S(1)}, f32[250,4,20,2]{0,3,2,1:T(2,128)S(1)}, u32[]{:S(2)}, u32[]{:S(2)}) collective-permute-start(f32[250,4,20,2]{0,3,2,1:T(2,128)S(1)} %get-tuple-element.9), channel_id=1, source_target_pairs={{1,0},{2,1},{3,2},{4,3},{5,4},{6,5},{7,6},{0,7},{9,8},{10,9},{11,1... | collective-permute-start | bytes 480008 | tf_op jit(solution)/shard_map/ppermute | solution.py:19
  63.0 1.4 reshape.56
  64.3 1.4 fusion.15
  66.4 1.2 collective-permute-start.5
  68.1 2.2 %collective-permute-done.3 = f32[250,4,20,2]{0,3,2,1:T(2,128)S(1)} collective-permute-done((f32[250,4,20,2]{0,3,2,1:T(2,128)S(1)}, f32[250,4,20,2]{0,3,2,1:T(2,128)S(1)}, u32[]{:S(2)}, u32[]{:S(2)}) %collective-permute-start.3) | collective-permute-done | bytes 160032 | tf_op jit(solution)/shard_map/ppermute | solution.py:19
  70.3 6.4 %pad_maximum_fusion = f32[250,4,20,132]{0,3,2,1:T(8,128)S(1)} fusion(f32[250,4,20,2]{0,3,2,1:T(2,128)S(1)} %collective-permute-done.3, f32[250,4,2,128]{0,3,2,1:T(8,128)S(1)} %copy.26, f32[250,4,16,128]{0,3,2,1:T(8,128)} %copy.25, f32[250,4,2,128]{0,3,2,1:T(8,128)S(1)} %copy.24, f32[250,4,20,2]{0,3,2,1:T(2,128)S(1)} %collective-permute-done.2), kind=kLoop, calls=%fused_computation.1 | loop fusion | flops 10560000 | bytes 21120000 | tf_op jit(solution)/shard_map/concatenate | solution.py:20
  76.9 4.7 %collective-permute-start.7 = (f32[2,4,20,2]{3,2,1,0:T(8,128)S(1)}, f32[2,4,20,2]{3,2,1,0:T(8,128)S(1)}, u32[]{:S(2)}, u32[]{:S(2)}) collective-permute-start(f32[2,4,20,2]{3,2,1,0:T(8,128)S(1)} %get-tuple-element.27), channel_id=1, source_target_pairs={{1,0},{2,1},{3,2},{4,3},{5,4},{6,5},{7,6},{0,7},{9,8},{10,9},{11,1... | collective-permute-start | bytes 3848 | tf_op jit(solution)/shard_map/ppermute | solution.py:19
  81.7 2.6 %collective-permute-done.6 = f32[2,4,20,2]{3,2,1,0:T(8,128)S(1)} collective-permute-done((f32[2,4,20,2]{3,2,1,0:T(8,128)S(1)}, f32[2,4,20,2]{3,2,1,0:T(8,128)S(1)}, u32[]{:S(2)}, u32[]{:S(2)}) %collective-permute-start.6) | collective-permute-done | bytes 1312 | tf_op jit(solution)/shard_map/ppermute | solution.py:16
  84.9 5.7 %fusion = f32[250,4,19,130]{0,3,2,1:T(8,128)} fusion(f32[250,4,20,132]{0,3,2,1:T(8,128)S(1)} %pad_maximum_fusion, f32[4,19,130]{2,1,0:T(8,128)S(1)} %get-tuple-element.23, f32[4,19,130]{2,1,0:T(8,128)S(1)} %get-tuple-element.22), kind=kLoop, calls=%fused_computation.3 | loop fusion | flops 7410000 | bytes 29719040 | tf_op jit(solution)/shard_map/add | solution.py:77
  90.5 6.4 %fusion.2 = f32[250,4,18,131]{0,3,2,1:T(8,128)} fusion(f32[250,4,20,132]{0,3,2,1:T(8,128)S(1)} %pad_maximum_fusion, f32[4,18,131]{2,1,0:T(8,128)S(1)} %get-tuple-element.25, f32[4,18,131]{2,1,0:T(8,128)S(1)} %get-tuple-element.24), kind=kLoop, calls=%fused_computation.8 | loop fusion | flops 7074000 | bytes 28371456 | tf_op jit(solution)/shard_map/add | solution.py:81
  96.9 17.9 %fusion.1 = f32[250,4,18,130]{0,3,2,1:T(8,128)} fusion(f32[250,4,18,131]{0,3,2,1:T(8,128)} %fusion.2, f32[250,4,19,130]{0,3,2,1:T(8,128)} %fusion, f32[250,4,20,132]{0,3,2,1:T(8,128)S(1)} %pad_maximum_fusion), kind=kLoop, calls=%fused_computation.6 | loop fusion | flops 9360000 | bytes 56160000 | tf_op jit(solution)/shard_map/sub | solution.py:85
  114.8 11.4 %fusion.5 = f32[250,4,17,128]{0,3,2,1:T(8,128)} fusion(f32[250,4,18,130]{0,3,2,1:T(8,128)} %fusion.1, f32[4,17,128]{2,1,0:T(8,128)S(1)} %get-tuple-element.19, f32[4,17,128]{2,1,0:T(8,128)S(1)} %get-tuple-element.18), kind=kLoop, calls=%fused_computation.16 | loop fusion | flops 6528000 | bytes 26181632 | tf_op jit(solution)/shard_map/add | solution.py:77
  127.3 4.8 %fusion.4 = f32[250,4,16,129]{0,3,2,1:T(8,128)} fusion(f32[250,4,18,130]{0,3,2,1:T(8,128)S(1)} %bitcast.43, f32[4,16,129]{2,1,0:T(8,128)S(1)} %get-tuple-element.21, f32[4,16,129]{2,1,0:T(8,128)S(1)} %get-tuple-element.20), kind=kLoop, calls=%fused_computation.13 | loop fusion | flops 6192000 | bytes 24834048 | tf_op jit(solution)/shard_map/add | solution.py:81
  132.2 22.5 %fusion.7 = f32[250,4,16,128]{0,3,2,1:T(8,128)} fusion(f32[250,4,16,129]{0,3,2,1:T(8,128)} %fusion.4, f32[250,4,17,128]{0,3,2,1:T(8,128)} %fusion.5, f32[250,4,18,130]{0,3,2,1:T(8,128)} %fusion.1, f32[4,16,128]{2,1,0:T(8,128)S(1)} %fusion.10, f32[250]{0:T(256)S(1)} %copy-done.4, f32[12,4,16,128]{3,2,1,0:T(8,128)S(1)} %bitcast.47, f32[250,12]{0,1:T(8,128)S(1)} %copy-done.3), kind=kOutput, calls=%fused_computation.19 | convolution fusion | flops 323584000 | bytes 49590984 | tf_op jit(solution)/shard_map/sf,flxy->slxy/dot_general | solution.py:92
  154.7 10.0 %copy.28 = f32[250,4,16,128]{3,2,1,0:T(8,128)} copy(f32[250,4,16,128]{0,3,2,1:T(8,128)} %fusion.7) | data formatting | bytes 16384000
  (46 shorter events, 5.6 us)
Async XLA Ops:
  0.6 11.3 %copy-start = (bf16[64,128,128]{2,1,0:T(8,128)(2,1)S(1)}, bf16[64,128,128]{2,1,0:T(8,128)(2,1)}, u32[]{:S(2)}) copy-start(bf16[64,128,128]{2,1,0:T(8,128)(2,1)} %param.8) | copy-start | bytes 6291460
  4.7 14.3 %all-to-all-start.1 = ((bf16[32,2,1]{1,2,0:T(2,128)(2,1)}), bf16[32,2,1]{1,2,0:T(2,128)(2,1)S(1)}, u32[]{:S(2)}, u32[]{:S(2)}) async-start(bf16[32,2,1]{1,2,0:T(2,128)(2,1)} %all_to_all.16), calls=%async_computation.1 | async-start | bytes 32768 | tf_op jit(solution)/shard_map/all_to_all | solution.py:27
  19.0 44.0 %all-to-all-start = ((bf16[32,2,6144]{2,1,0:T(2,128)(2,1)}), bf16[32,2,6144]{2,1,0:T(2,128)(2,1)S(1)}, u32[]{:S(2)}, u32[]{:S(2)}) async-start(bf16[32,2,6144]{2,1,0:T(2,128)(2,1)} %all_to_all.12), calls=%async_computation | async-start | bytes 1572864 | tf_op jit(solution)/shard_map/all_to_all | solution.py:26
  27.3 27.4 %collective-permute-start = (f32[250,4,2,128]{3,1,2,0:T(4,128)}, f32[250,4,2,128]{3,1,2,0:T(4,128)S(1)}, u32[]{:S(2)}, u32[]{:S(2)}) collective-permute-start(f32[250,4,2,128]{3,1,2,0:T(4,128)} %copy.30), channel_id=1, source_target_pairs={{0,8},{8,16},{16,24},{24,0},{1,9},{9,17},{17,25},{25,1},{2,10},{10... | collective-permute-start | bytes 3072008 | tf_op jit(solution)/shard_map/ppermute | solution.py:16
  28.6 26.6 %collective-permute-start.1 = (f32[250,4,2,128]{3,1,2,0:T(4,128)}, f32[250,4,2,128]{3,1,2,0:T(4,128)}, u32[]{:S(2)}, u32[]{:S(2)}) collective-permute-start(f32[250,4,2,128]{3,1,2,0:T(4,128)} %copy.31), channel_id=1, source_target_pairs={{8,0},{16,8},{24,16},{0,24},{9,1},{17,9},{25,17},{1,25},{10,2},{18... | collective-permute-start | bytes 3072008 | tf_op jit(solution)/shard_map/ppermute | solution.py:19
  58.2 9.9 %collective-permute-start.2 = (f32[250,4,20,2]{0,3,2,1:T(2,128)S(1)}, f32[250,4,20,2]{0,3,2,1:T(2,128)S(1)}, u32[]{:S(2)}, u32[]{:S(2)}) collective-permute-start(f32[250,4,20,2]{0,3,2,1:T(2,128)S(1)} %get-tuple-element.8), channel_id=1, source_target_pairs={{0,1},{1,2},{2,3},{3,4},{4,5},{5,6},{6,7},{7,0},{8,9},{9,10},{10,1... | collective-permute-start | bytes 480008 | tf_op jit(solution)/shard_map/ppermute | solution.py:16
  59.8 10.5 %collective-permute-start.3 = (f32[250,4,20,2]{0,3,2,1:T(2,128)S(1)}, f32[250,4,20,2]{0,3,2,1:T(2,128)S(1)}, u32[]{:S(2)}, u32[]{:S(2)}) collective-permute-start(f32[250,4,20,2]{0,3,2,1:T(2,128)S(1)} %get-tuple-element.9), channel_id=1, source_target_pairs={{1,0},{2,1},{3,2},{4,3},{5,4},{6,5},{7,6},{0,7},{9,8},{10,9},{11,1... | collective-permute-start | bytes 480008 | tf_op jit(solution)/shard_map/ppermute | solution.py:19
  65.8 66.4 %copy-start.2 = (f32[48,128,16]{1,2,0:T(8,128)}, f32[48,128,16]{1,2,0:T(8,128)S(1)}, u32[]{:S(2)}) copy-start(f32[48,128,16]{1,2,0:T(8,128)S(1)} %fusion.15) | copy-start | bytes 1179652
  65.8 10.9 %collective-permute-start.4 = (f32[2,4,2,128]{3,2,1,0:T(2,128)S(1)}, f32[2,4,2,128]{3,2,1,0:T(2,128)S(1)}, u32[]{:S(2)}, u32[]{:S(2)}) collective-permute-start(f32[2,4,2,128]{3,2,1,0:T(2,128)S(1)} %get-tuple-element.28), channel_id=1, source_target_pairs={{0,8},{8,16},{16,24},{24,0},{1,9},{9,17},{17,25},{25,1},{2,10},{10... | collective-permute-start | bytes 24584 | tf_op jit(solution)/shard_map/ppermute | solution.py:16
  66.4 10.4 %collective-permute-start.5 = (f32[2,4,2,128]{3,2,1,0:T(2,128)S(1)}, f32[2,4,2,128]{3,2,1,0:T(2,128)S(1)}, u32[]{:S(2)}, u32[]{:S(2)}) collective-permute-start(f32[2,4,2,128]{3,2,1,0:T(2,128)S(1)} %get-tuple-element.29), channel_id=1, source_target_pairs={{8,0},{16,8},{24,16},{0,24},{9,1},{17,9},{25,17},{1,25},{10,2},{18... | collective-permute-start | bytes 24584 | tf_op jit(solution)/shard_map/ppermute | solution.py:19
  76.9 7.5 %collective-permute-start.6 = (f32[2,4,20,2]{3,2,1,0:T(8,128)S(1)}, f32[2,4,20,2]{3,2,1,0:T(8,128)S(1)}, u32[]{:S(2)}, u32[]{:S(2)}) collective-permute-start(f32[2,4,20,2]{3,2,1,0:T(8,128)S(1)} %get-tuple-element.26), channel_id=1, source_target_pairs={{0,1},{1,2},{2,3},{3,4},{4,5},{5,6},{6,7},{7,0},{8,9},{9,10},{10,1... | collective-permute-start | bytes 3848 | tf_op jit(solution)/shard_map/ppermute | solution.py:16
  76.9 7.4 %collective-permute-start.7 = (f32[2,4,20,2]{3,2,1,0:T(8,128)S(1)}, f32[2,4,20,2]{3,2,1,0:T(8,128)S(1)}, u32[]{:S(2)}, u32[]{:S(2)}) collective-permute-start(f32[2,4,20,2]{3,2,1,0:T(8,128)S(1)} %get-tuple-element.27), channel_id=1, source_target_pairs={{1,0},{2,1},{3,2},{4,3},{5,4},{6,5},{7,6},{0,7},{9,8},{10,9},{11,1... | collective-permute-start | bytes 3848 | tf_op jit(solution)/shard_map/ppermute | solution.py:19
  114.8 11.4 %slice-start = ((s8[10027008]{0:T(1024)(128)(4,1)}), s8[4194304]{0:T(1024)(128)(4,1)S(1)}, s32[]{:S(2)}) async-start(s8[10027008]{0:T(1024)(128)(4,1)} %bitcast.42), calls=%async_computation.2 | async-start | bytes 8388608
  114.8 12.0 %slice-start.1 = ((s8[10027008]{0:T(1024)(128)(4,1)}), s8[4194304]{0:T(1024)(128)(4,1)S(1)}, s32[]{:S(2)}) async-start(s8[10027008]{0:T(1024)(128)(4,1)} %bitcast.42), calls=%async_computation.3 | async-start | bytes 8388608
  114.8 12.6 %slice-start.2 = ((s8[10027008]{0:T(1024)(128)(4,1)}), s8[1638400]{0:T(1024)(128)(4,1)S(1)}, s32[]{:S(2)}) async-start(s8[10027008]{0:T(1024)(128)(4,1)} %bitcast.42), calls=%async_computation.4 | async-start | bytes 3276800
  127.3 4.8 %copy-start.3 = (f32[250,12]{0,1:T(8,128)S(1)}, f32[250,12]{0,1:T(8,128)}, u32[]{:S(2)}) copy-start(f32[250,12]{0,1:T(8,128)} %param.12) | copy-start | bytes 36004
  127.3 4.8 %copy-start.4 = (f32[250]{0:T(256)S(1)}, f32[250]{0:T(256)}, u32[]{:S(2)}) copy-start(f32[250]{0:T(256)} %param.13) | copy-start | bytes 3004
  132.2 32.5 %copy-start.1 = (bf16[64,128,128]{2,1,0:T(8,128)(2,1)S(1)}, bf16[64,128,128]{2,1,0:T(8,128)(2,1)}, u32[]{:S(2)}) copy-start(bf16[64,128,128]{2,1,0:T(8,128)(2,1)} %param.8) | copy-start | bytes 6291460
where the time goes:
time: 166 us; the launch traced here: 165 us
  other arithmetic  56.9 us (34%)
  local copies, waits for them, and re-layouts  33.9 us (20%)
  matrix products  26.9 us (16%)
  waiting for transfers between devices  23.1 us (14%)
  starting transfers between devices  23 us (14%)
    unnamed x20, local copies, waits for them, and re-layouts  23.6 us
    dot_general x1, matrix products, local(): jnp.einsum('sf,flxy->slxy', rate_coef, met_tile, precision=lax.Precision....  22.5 us
    sub x1, other arithmetic, local(): amount[:, :, 1:-1, 1:-1] - (flux_x[:, :, 1:, :] - flux_x[:, :, :-1, :])  17.9 us
    ppermute x4, waiting for transfers between devices, with_halo(): lax.ppermute(lax.slice_in_dim(block, block.shape[dim] - width, None, axis...  17.4 us
    add x2, other arithmetic, local(): jnp.maximum(wind_x[:, :-1, 1:-1], 0.0) * amount[:, :, :-1, 1:-1]  17.1 us
    add x2, other arithmetic, local(): jnp.maximum(wind_y[:, 1:-1, :-1], 0.0) * amount[:, :, 1:-1, :-1]  11.2 us
    ppermute x4, starting transfers between devices, with_halo(): lax.ppermute(lax.slice_in_dim(block, 0, width, axis=dim), axis, backward)  10.8 us
    all_to_all x1, starting transfers between devices, deliver(): lax.all_to_all(slot_label, ('face', 'tile'), split_axis=0, concat_axis=0,...  7.3 us
  transfers between devices with their start and end apart: 10, of which 5 were waited for; matrix products, arithmetic and copies ran while one was open for 19% of the time, Pallas kernels for 0%

commit v1 on v0

v1 whole, which is shorter than its diff:
```python
import functools

import jax
import jax.numpy as jnp
from jax import lax
from jax.experimental import pallas as pl
from jax.experimental.pallas import tpu as pltpu
from jax.sharding import PartitionSpec as P

CAP = 2
F32 = jnp.float32
BF16 = jnp.bfloat16
HALF = 128
ROW_GROUP = 4
BIG = 50
BIGGEST = 60
MIB = 1024 * 1024
SMEM = pltpu.MemorySpace.SMEM


def here(count):
    return [pl.BlockSpec(memory_space=pl.ANY)] * count


def params(mib):
    return pltpu.CompilerParams(vmem_limit_bytes=mib * MIB)


def buffers(arrays):
    return [pltpu.VMEM(x.shape, x.dtype) for x in arrays]


def fetch(sources, targets, sems):
    copies = [pltpu.make_async_copy(s, t, sems.at[i]) for i, (s, t) in enumerate(zip(sources, targets))]
    for copy in copies:
        copy.start()
    return copies


def finish(copies):
    for copy in copies:
        copy.wait()


def lanes(shape):
    return lax.broadcasted_iota(jnp.int32, shape, len(shape) - 1)


def sublanes(shape):
    return lax.broadcasted_iota(jnp.int32, shape, len(shape) - 2)


def turn(x, shift):
    count = x.shape[-1]
    shift = shift % count
    return x if shift == 0 else pltpu.roll(x, shift, x.ndim - 1)


def regrid_kernel(rows, dest_any, row_any, src_any, weight_any, tracer_any,
                  first_any, second_any, top_any, bottom_any,
                  dest_ref, row_ref, src_ref, weight_ref, first_ref, second_ref, border, top_ref, bottom_ref,
                  index_ref, count_ref, sems, border_sems):
    owners = first_ref.shape[0]
    levels = top_ref.shape[1]
    species = tracer_any.shape[0]
    blocks, levfields, cells = src_ref.shape
    copies = fetch([dest_any, row_any, src_any, weight_any], [dest_ref, row_ref, src_ref, weight_ref], sems)
    wanted = [(level, row) for level in range(levels) for row in (0, 1, rows - 2, rows - 1)]
    lines = fetch(
        [tracer_any.at[:, level * rows + row, 0, :] for level, row in wanted],
        [border.at[i, pl.ds(0, species), :] for i in range(len(wanted))], border_sems,
    )

    def clear(d, carry):
        count_ref[d] = 0
        for k in range(CAP):
            index_ref[d * CAP + k] = -1
        return carry

    lax.fori_loop(0, owners, clear, 0, unroll=8)
    finish(copies[:2])

    def place(b, carry):
        d = dest_ref[b]
        k = count_ref[d]
        index_ref[d * CAP + jnp.minimum(k, CAP - 1)] = b
        count_ref[d] = k + 1
        return carry

    lax.fori_loop(0, blocks, place, 0, unroll=8)
    finish(copies[2:])
    row_id = sublanes((16, cells))
    low_half = sublanes((8, cells)) < 4

    def send(d, carry):
        parts, heads = [], []
        for k in range(CAP):
            b = index_ref[d * CAP + k]
            used = b >= 0
            at = jnp.maximum(b, 0)
            product = jnp.dot(src_ref[at], weight_ref[at], preferred_element_type=F32)
            product = jnp.where(used, product, 0.0)
            label = jnp.where(used, row_ref[at], -1).astype(F32)
            parts.append(product)
            heads.append(jnp.where(row_id < 12, product[0:16], label))
        first_ref[d] = jnp.concatenate(heads, axis=0).astype(BF16)
        mixed = jnp.where(low_half, pltpu.roll(parts[0][8:16], 4, 0), parts[1][8:16])
        second_ref[d] = jnp.concatenate([parts[0][16:], parts[1][16:], mixed], axis=0).astype(BF16)
        return carry

    lax.fori_loop(0, owners, send, 0, unroll=8)
    copies = fetch([first_ref, second_ref], [first_any, second_any], sems)
    finish(lines)
    for i, (level, row) in enumerate(wanted):
        if row < 2:
            top_ref[row, level] = border[i].astype(BF16)
        else:
            bottom_ref[row - rows + 2, level] = border[i].astype(BF16)
    finish(copies + fetch([top_ref, bottom_ref], [top_any, bottom_any], border_sems))


def regrid(block_dest, block_row, met_src, weights, planes, owners, padded, levels, rows):
    blocks, levfields, cells = met_src.shape
    line = jax.ShapeDtypeStruct((2, levels, padded, cells), BF16)
    first = jax.ShapeDtypeStruct((owners, CAP * 16, cells), BF16)
    second = jax.ShapeDtypeStruct((owners, CAP * (levfields - 12), cells), BF16)
    return pl.pallas_call(
        functools.partial(regrid_kernel, rows),
        out_shape=(first, second, line, line),
        in_specs=here(5),
        out_specs=tuple(here(4)),
        scratch_shapes=[
            pltpu.SMEM(block_dest.shape, jnp.int32), pltpu.SMEM(block_row.shape, jnp.int32),
            *buffers([met_src, weights, first, second]),
            pltpu.VMEM((4 * levels, padded, cells), F32), *buffers([line, line]),
            pltpu.SMEM((owners * CAP,), jnp.int32), pltpu.SMEM((owners,), jnp.int32),
            pltpu.SemaphoreType.DMA((4,)), pltpu.SemaphoreType.DMA((4 * levels,)),
        ],
        compiler_params=params(BIGGEST),
        cost_estimate=pl.CostEstimate(
            flops=2 * blocks * levfields * cells * cells, bytes_accessed=6 * MIB, transcendentals=0
        ),
        name="regrid",
    )(block_dest, block_row, met_src, weights, planes)


def load_planes(source, target, sems):
    species = source.shape[0]
    copies = []
    for k in range(source.shape[1]):
        copy = pltpu.make_async_copy(source.at[:, k, 0, :], target.at[k, pl.ds(0, species), :], sems.at[k])
        copy.start()
        copies.append(copy)
    return copies


def column_kernel(levels, tracer_any, right_ref, left_ref, planes, total, picker, sems):
    count, padded, cells = planes.shape
    rows = count // levels
    load_planes(tracer_any, planes, sems)
    total[...] = jnp.zeros_like(total)
    picker[...] = jnp.zeros_like(picker)
    sub, lane = sublanes((16, 2 * cells)), lanes((16, 2 * cells))

    def one_level(level, carry):
        for row in range(rows):
            pltpu.make_async_copy(
                tracer_any.at[:, level * rows + row, 0, :],
                planes.at[level * rows + row, pl.ds(0, tracer_any.shape[0]), :],
                sems.at[level * rows + row],
            ).wait()
        for row in range(0, rows, 2):
            pair = []
            for h in range(2):
                k = level * rows + row + h
                pair.append(planes[k].astype(BF16))
                low = (sub < 2) & (lane == cells + 2 * k + sub)
                high = (sub >= 14) & (lane == 2 * k + sub - 14)
                picker[row // 2, pl.ds(h * cells, 16), :] = jnp.where(low, 1.0, 0.0).astype(BF16)
                picker[row // 2, pl.ds((h + 1) * cells - 16, 16), :] = jnp.where(high, 1.0, 0.0).astype(BF16)
            both = jnp.concatenate(pair, axis=1)
            total[...] += jnp.dot(both, picker[row // 2], preferred_element_type=F32)
        return carry

    lax.fori_loop(0, levels, one_level, 0)
    right_ref[...] = total[:, 0:cells].astype(BF16)
    left_ref[...] = total[:, cells:].astype(BF16)


def columns(planes, padded, levels):
    _, count, _, cells = planes.shape
    side = jax.ShapeDtypeStruct((padded, cells), BF16)
    return pl.pallas_call(
        functools.partial(column_kernel, levels),
        out_shape=(side, side),
        in_specs=here(1),
        scratch_shapes=[
            pltpu.VMEM((count, padded, cells), F32),
            pltpu.VMEM((padded, 2 * cells), F32), pltpu.VMEM((count // levels // 2, 2 * cells, 2 * cells), BF16),
            pltpu.SemaphoreType.DMA((count,)),
        ],
        compiler_params=params(BIG),
        cost_estimate=pl.CostEstimate(flops=12 * planes.size, bytes_accessed=4 * planes.size, transcendentals=0),
        name="columns",
    )(planes)


def softplus(x):
    return jnp.maximum(x, 0.0) + jnp.log(1.0 + jnp.exp(-jnp.abs(x)))


def first_fields_kernel(levels, first_any, met_any, courant_any, last_any, zero_any, light_any, label_ref,
                        first_ref, met_ref, courant_ref, light_ref, label_v, label_s, sems):
    owners, _, cells = first_ref.shape
    rows = met_ref.shape[0]
    finish(fetch([first_any], [first_ref], sems))

    def gather(d, carry):
        x = first_ref[d].astype(F32)
        found = [x[16 * k + 12 : 16 * k + 13] for k in range(CAP)]
        label_v[pl.ds(d * CAP, CAP), :] = jnp.concatenate(found, axis=0).astype(jnp.int32)
        return carry

    lax.fori_loop(0, owners, gather, 0, unroll=8)
    labels = fetch([label_v], [label_s], sems)
    keep = sublanes((16, cells)) < 12

    def add(d, sums):
        x = first_ref[d].astype(F32)
        sums = list(sums)
        for k in range(CAP):
            part = jnp.where(keep, x[16 * k : 16 * k + 16], 0.0)
            label = jnp.broadcast_to(x[16 * k + 12 : 16 * k + 13], (16, cells))
            for r in range(rows):
                sums[r] += jnp.where(label == r, part, 0.0)
        return tuple(sums)

    zero = jnp.zeros((16, cells), F32)
    sums = lax.fori_loop(0, owners, add, (zero,) * rows)
    for r in range(rows):
        met_ref[r] = sums[r]
        courant_ref[r] = 0.3 * jnp.tanh(sums[r][0 : 2 * levels])
    copies = fetch(
        [courant_ref, courant_ref.at[pl.ds(rows - 2, 2)], courant_ref.at[pl.ds(0, 1)], met_ref],
        [courant_any, last_any, zero_any, met_any], sems.at[pl.ds(1, 4)],
    )
    depth = softplus(met_ref[:, 2 * levels : 4 * levels, :])
    parts = []
    running = jnp.zeros((rows, 1, cells), F32)
    for level in range(levels):
        running = running + depth[:, level : level + 1]
        parts.append(jnp.exp(-running))
    parts.append(jnp.zeros((rows, 8 - levels, cells), F32))
    light_ref[...] = jnp.concatenate(parts, axis=1)
    finish(labels)
    copies += fetch([light_ref], [light_any], sems)

    def keep_label(i, carry):
        label = label_s[i, 0]
        label_ref[i] = jnp.where(label < 0, rows, label)
        return carry

    lax.fori_loop(0, owners * CAP, keep_label, 0, unroll=8)
    finish(copies)


def first_fields(first, levels, rows):
    owners, _, cells = first.shape
    outs = (
        jax.ShapeDtypeStruct((rows, 16, cells), F32),
        jax.ShapeDtypeStruct((rows, 2 * levels, cells), F32),
        jax.ShapeDtypeStruct((rows, 8, cells), F32),
    )
    last = jax.ShapeDtypeStruct((2, 2 * levels, cells), F32)
    zero = jax.ShapeDtypeStruct((1, 2 * levels, cells), F32)
    return pl.pallas_call(
        functools.partial(first_fields_kernel, levels),
        out_shape=(outs[0], outs[1], last, zero, outs[2], jax.ShapeDtypeStruct((owners * CAP,), jnp.int32)),
        in_specs=here(1),
        out_specs=(*here(5), pl.BlockSpec(memory_space=SMEM)),
        scratch_shapes=[
            *buffers([first, *outs]),
            pltpu.VMEM((owners * CAP, cells), jnp.int32),
            pltpu.SMEM((owners * CAP, cells), jnp.int32),
            pltpu.SemaphoreType.DMA((5,)),
        ],
        compiler_params=params(6),
        cost_estimate=pl.CostEstimate(flops=MIB, bytes_accessed=2 * MIB, transcendentals=MIB // 8),
        name="first_fields",
    )(first)


def ghost_lines(courant_ref, below_ref, above_ref):
    rows = courant_ref.shape[0]
    return [below_ref[0], below_ref[1]] + [courant_ref[r] for r in range(rows)] + [above_ref[0]]


def edge_kernel(below_any, above_any, right_any, left_any, courant_any, cbelow_any, cabove_any,
                right_out, left_out, cright_out,
                below_ref, above_ref, right_two, left_two, courant_ref, cbelow_ref, cabove_ref, cright_ref, sems):
    levels, padded, cells = below_ref.shape
    fields = cright_ref.shape[0]
    span = cells // levels
    copies = fetch(
        [courant_any, cbelow_any, cabove_any, below_any.at[1], above_any.at[0], right_any, left_any],
        [courant_ref, cbelow_ref, cabove_ref, below_ref, above_ref,
         right_two.at[pl.ds(0, padded)], left_two.at[pl.ds(0, padded)]], sems,
    )
    finish(copies[:3])
    pair = lanes((fields, cells)) // 2
    right = jnp.zeros((fields, cells), F32)
    left = jnp.zeros((fields, cells), F32)
    for k, x in enumerate(ghost_lines(courant_ref, cbelow_ref, cabove_ref)):
        moved = turn(x, 2 * k - (cells - 2))
        right = jnp.where(pair == k, moved, right)
        left = jnp.where(pair == k + 1, moved, left)
    left = turn(left, -2)
    cright_ref[...] = right
    for ref, x in ((right_two, right), (left_two, left)):
        high = x.astype(BF16).astype(F32)
        ref[pl.ds(2 * padded, 2 * fields), :] = jnp.concatenate([high, x - high], axis=0).astype(BF16)
    finish(copies[3:])
    pair = lanes((padded, cells)) // 2
    corner_right = jnp.zeros((padded, cells), F32)
    corner_left = jnp.zeros((padded, cells), F32)
    for level in range(levels):
        for ref, k in ((below_ref, level * span // 2), (above_ref, (level + 1) * span // 2 - 1)):
            moved = turn(ref[level].astype(F32), 2 * k - (cells - 2))
            corner_right = jnp.where(pair == k, moved, corner_right)
            corner_left = jnp.where(pair == (k + 1) % (cells // 2), moved, corner_left)
    right_two[pl.ds(padded, padded), :] = corner_right.astype(BF16)
    left_two[pl.ds(padded, padded), :] = turn(corner_left, -2).astype(BF16)
    finish(fetch([right_two, left_two, cright_ref], [right_out, left_out, cright_out], sems))


def edges(below, above, right, left, courant, cbelow, cabove):
    levels, padded, cells = below.shape[1:]
    fields = courant.shape[1]
    side = jax.ShapeDtypeStruct((2 * padded + 2 * fields, cells), BF16)
    line = jax.ShapeDtypeStruct((levels, padded, cells), BF16)
    own = jax.ShapeDtypeStruct((fields, cells), F32)
    return pl.pallas_call(
        edge_kernel,
        out_shape=(side, side, own),
        in_specs=here(7),
        out_specs=tuple(here(3)),
        scratch_shapes=[
            *buffers([line, line, side, side, courant, cbelow, cabove, own]), pltpu.SemaphoreType.DMA((7,))
        ],
        compiler_params=params(8),
        cost_estimate=pl.CostEstimate(flops=below.size, bytes_accessed=2 * MIB, transcendentals=0),
        name="edges",
    )(below, above, right, left, courant, cbelow, cabove)


def five_weights(face_x, face_x_low, face_y, face_y_low):
    up = -jnp.minimum(face_x, 0.0)
    down = jnp.maximum(face_x_low, 0.0)
    right = -jnp.minimum(face_y, 0.0)
    left = jnp.maximum(face_y_low, 0.0)
    stay = (
        1.0
        - (jnp.maximum(face_x, 0.0) - jnp.minimum(face_x_low, 0.0))
        - (jnp.maximum(face_y, 0.0) - jnp.minimum(face_y_low, 0.0))
    )
    return stay, up, down, left, right


def spread(x, level, count):
    return jnp.broadcast_to(x[level : level + 1], (count, x.shape[1]))


def make_weights(levels, courant_ref, below_ref, above_ref, own_right, west, east, inner, side, edge):
    rows, fields, cells = courant_ref.shape
    lane = lanes((fields, cells))
    line = ghost_lines(courant_ref, below_ref, above_ref)
    for i in range(1, rows + 3):
        now, low = line[i], line[i - 1]
        face_y_low = jnp.where(lane == 0, turn(west, -(2 * i + 1)), turn(now, 1))[levels:]
        five = five_weights(now[:levels], low[:levels], now[levels:], face_y_low)
        for level in range(levels):
            for c in range(3):
                inner[level, i - 1, c] = spread(five[c], level, 8)
            for c in range(2):
                side[level, i - 1, c] = spread(five[3 + c], level, 16).astype(BF16)
    odd = lane % 2 == 1
    middle = jnp.where(odd, west, east)
    lower = turn(middle, 2)
    y_low = jnp.where(odd, turn(west, 1), turn(own_right, -1))
    stay, up, down, left, right = five_weights(
        middle[:levels], lower[:levels], middle[levels:], y_low[levels:]
    )
    odd = odd[:levels]
    outer_w = jnp.where(odd, left, right)
    inner_w = jnp.where(odd, right, left)
    lane8 = lanes((8, cells))
    span = cells // levels
    for c, x in enumerate((stay, up, down, outer_w, inner_w)):
        out = jnp.zeros((8, cells), F32)
        for level in range(levels):
            out = jnp.where(lane8 // span == level, turn(spread(x, level, 8), level * span - 4), out)
        edge[c] = out


def side_columns(rows, levels, right_ref, left_ref, west_ref, east_ref, edge, mid_ref, corner_ref, next_ref):
    padded, cells = right_ref.shape
    span = cells // levels
    lane = lanes((16, cells))
    odd = lane % 2 == 1
    row_of = (lane % span) // 2

    def group(g, carry):
        part = pl.ds(pl.multiple_of(g * 16, 16), 16)
        corner_part = pl.ds(pl.multiple_of(padded + g * 16, 16), 16)
        lo, lo_c = west_ref[part, :].astype(F32), west_ref[corner_part, :].astype(F32)
        hi, hi_c = east_ref[part, :].astype(F32), east_ref[corner_part, :].astype(F32)
        own_r, own_l = right_ref[part, :].astype(F32), left_ref[part, :].astype(F32)
        weights = [jnp.concatenate([edge[c]] * 2, axis=0) for c in range(5)]
        mid = jnp.where(odd, lo, hi)
        corner = jnp.where(odd, lo_c, hi_c)
        outside = jnp.where(odd, turn(lo, 1), turn(hi, -1))
        inside = jnp.where(odd, turn(own_l, 1), turn(own_r, -1))
        above = jnp.where(row_of == rows - 1, corner, turn(mid, -2))
        below = jnp.where(row_of == 0, corner, turn(mid, 2))
        mid_ref[part, :] = mid.astype(BF16)
        corner_ref[part, :] = corner.astype(BF16)
        after = (
            weights[0] * mid + weights[1] * above + weights[2] * below
            + weights[3] * outside + weights[4] * inside
        )
        next_ref[part, :] = after.astype(BF16)
        return carry

    lax.fori_loop(0, padded // 16, group, 0)


def advect_kernel(
    levels, tracer_any, below_any, above_any, right_any, left_any, west_any, east_any,
    courant_any, cbelow_any, cabove_any, cright_any, out_any,
    planes, below_ref, above_ref, right_ref, left_ref, west_ref, east_ref,
    courant_ref, cbelow_ref, cabove_ref, cright_ref,
    inner, side, edge, mid_ref, corner_ref, next_ref, matrix, low_mask, high_mask, once, once16,
    plane_sems, in_sems, out_sems,
):
    rows, _, cells = courant_ref.shape
    padded = planes.shape[1]
    span = cells // levels
    small = fetch(
        [courant_any, cbelow_any, cabove_any, cright_any, west_any, east_any,
         right_any, left_any, below_any, above_any],
        [courant_ref, cbelow_ref, cabove_ref, cright_ref, west_ref, east_ref,
         right_ref, left_ref, below_ref, above_ref], in_sems,
    )
    loads = load_planes(tracer_any, planes, plane_sems)
    sub, lane = sublanes((cells, cells)), lanes((cells, cells))
    low_mask[...] = jnp.where(sub == lane - 1, 1.0, 0.0).astype(BF16)
    high_mask[...] = jnp.where(sub == lane + 1, 1.0, 0.0).astype(BF16)
    finish(small[:6])
    fields = cright_ref.shape[0]
    cwest, ceast = (
        ref[pl.ds(2 * padded, fields), :].astype(F32) + ref[pl.ds(2 * padded + fields, fields), :].astype(F32)
        for ref in (west_ref, east_ref)
    )
    make_weights(levels, courant_ref, cbelow_ref, cabove_ref, cright_ref[...], cwest, ceast, inner, side, edge)
    finish(small[6:])
    side_columns(rows, levels, right_ref, left_ref, west_ref, east_ref, edge, mid_ref, corner_ref, next_ref)
    sub16, lane16 = sublanes((16, cells)), lanes((16, cells))

    def set_matrix(level, i):
        left, right = side[level, i + 1, 0], side[level, i + 1, 1]
        for t in range(cells // 16):
            at = pl.ds(16 * t, 16)
            matrix[i + 1, at, :] = low_mask[at, :] * left + high_mask[at, :] * right
        matrix[i + 1, pl.ds(cells, cells), :] = jnp.zeros((cells, cells), BF16)
        p = 2 * min(max(i, 0), rows - 1)
        tile = jnp.where(
            (sub16 == p % 16 + 1) & (lane16 == 0), left.astype(F32),
            jnp.where((sub16 == p % 16) & (lane16 == cells - 1), right.astype(F32), 0.0),
        )
        at = pl.multiple_of(cells + level * span + p // 16 * 16, 16)
        matrix[i + 1, pl.ds(at, 16), :] = tile.astype(BF16)

    def weighted(weights, x, up, down):
        count = x.shape[0] // 8
        stay, up_w, down_w = (w[None] for w in weights)
        x, up, down = (v.reshape(count, 8, cells) for v in (x, up, down))
        return (stay * x + up_w * up + down_w * down).reshape(count * 8, cells)

    def one_level(level, carry):
        for r in range(rows):
            pltpu.make_async_copy(
                tracer_any.at[:, level * rows + r, 0, :],
                planes.at[level * rows + r, pl.ds(0, tracer_any.shape[0]), :],
                plane_sems.at[level * rows + r],
            ).wait()
        for i in range(-1, rows + 1):
            set_matrix(level, i)

        def half(b, carry):
            part = pl.ds(pl.multiple_of(b * HALF, HALF), HALF)

            def before(i):
                if i < 0:
                    return below_ref[i + 2, level, part, :].astype(F32)
                if i >= rows:
                    return above_ref[i - rows, level, part, :].astype(F32)
                return planes[level * rows + i, part, :]

            for i in range(-1, rows + 1):
                x = before(i)
                beside = (mid_ref if 0 <= i < rows else corner_ref)[part, :]
                both = jnp.concatenate([x.astype(BF16), beside], axis=1)
                across = jnp.dot(both, matrix[i + 1], preferred_element_type=F32)
                weights = [inner[level, i + 1, c] for c in range(3)]
                x = weighted(weights, x, before(i + 1), before(i - 1)) + across
                once[i + 1] = x
                if 0 <= i < rows:
                    once16[i] = x.astype(BF16)
            for i in range(rows):
                both = jnp.concatenate([once16[i], next_ref[part, :]], axis=1)
                across = jnp.dot(both, matrix[i + 1], preferred_element_type=F32)
                weights = [inner[level, i + 1, c] for c in range(3)]
                planes[level * rows + i, part, :] = (
                    weighted(weights, once[i + 1], once[i + 2], once[i]) + across
                )
            return carry

        lax.fori_loop(0, padded // HALF, half, 0)
        for r in range(rows):
            pltpu.make_async_copy(
                planes.at[level * rows + r], out_any.at[level * rows + r], out_sems.at[level * rows + r]
            ).start()
        return carry

    lax.fori_loop(0, levels, one_level, 0)
    for k in range(levels * rows):
        pltpu.make_async_copy(planes.at[k], out_any.at[k], out_sems.at[k]).wait()


def advect(planes, below, above, right, left, west, east, courant, cbelow, cabove, cright):
    levels, padded, cells = below.shape[1:]
    rows = courant.shape[0]
    small = [below, above, right, left, west, east, courant, cbelow, cabove, cright]
    count = levels * rows
    column = pltpu.VMEM((padded, cells), BF16)
    square = pltpu.VMEM((cells, cells), BF16)
    return pl.pallas_call(
        functools.partial(advect_kernel, levels),
        out_shape=jax.ShapeDtypeStruct((count, padded, cells), F32),
        in_specs=here(1 + len(small)),
        out_specs=here(1)[0],
        scratch_shapes=[
            pltpu.VMEM((count, padded, cells), F32),
            *buffers(small),
            pltpu.VMEM((levels, rows + 2, 3, 8, cells), F32),
            pltpu.VMEM((levels, rows + 2, 2, 16, cells), BF16),
            pltpu.VMEM((5, 8, cells), F32),
            column, column, column,
            pltpu.VMEM((rows + 2, 2 * cells, cells), BF16),
            square, square,
            pltpu.VMEM((rows + 2, HALF, cells), F32),
            pltpu.VMEM((rows, HALF, cells), BF16),
            pltpu.SemaphoreType.DMA((count,)), pltpu.SemaphoreType.DMA((len(small),)),
            pltpu.SemaphoreType.DMA((count,)),
        ],
        compiler_params=params(BIG),
        cost_estimate=pl.CostEstimate(
            flops=40 * planes.size, bytes_accessed=8 * planes.size, transcendentals=0
        ),
        name="advect",
    )(planes, *small)


def chemistry_kernel(levels, label_any, second_any, met_any, light_any, rate_any, moved_any, out_any, tile_any,
                     label_ref, second_ref, met_ref, light_ref, rate_ref, planes, tile_ref, total, factor,
                     in_sems, plane_sems, out_sems):
    owners, _, cells = second_ref.shape
    count = planes.shape[0]
    rows = count // levels
    species = out_any.shape[0]
    levfields = total.shape[0] // (rows + 1)
    small = fetch(
        [label_any, second_any, met_any, light_any, rate_any],
        [label_ref, second_ref, met_ref, light_ref, rate_ref], in_sems,
    )
    for r in range(rows):
        for level in range(levels):
            k = level * rows + r
            pltpu.make_async_copy(moved_any.at[k], planes.at[k], plane_sems.at[k]).start()
    finish(small)
    for r in range(rows):
        total[pl.ds(r * levfields, 16), :] = met_ref[r]
        total[pl.ds(r * levfields + 16, levfields - 16), :] = jnp.zeros((levfields - 16, cells), F32)
    total[pl.ds(rows * levfields, levfields), :] = jnp.zeros((levfields, cells), F32)
    low_half = sublanes((8, cells)) < 4

    def add(d, carry):
        x = second_ref[d].astype(F32)
        many = levfields - 16
        mixed = x[CAP * many :]
        extra = [jnp.where(low_half, 0.0, pltpu.roll(mixed, 4, 0)), jnp.where(low_half, 0.0, mixed)]
        for k in range(CAP):
            at = pl.multiple_of(label_ref[d * CAP + k] * levfields, 8)
            total[pl.ds(at + 8, 8), :] += extra[k]
            total[pl.ds(at + 16, many), :] += x[k * many : (k + 1) * many]
        return carry

    lax.fori_loop(0, owners, add, 0, unroll=4)
    for r in range(rows):
        x = jnp.concatenate(
            [total[pl.ds(r * levfields, levfields), :], light_ref[r], jnp.zeros((8, cells), F32)], axis=0
        )
        high = x.astype(BF16)
        rest = (x - high.astype(F32)).astype(BF16)
        factor[r] = jnp.concatenate([high, rest, high], axis=0)

    def some_rows(c, carry):
        for dr in range(ROW_GROUP):
            for level in range(levels):
                k = level * rows + c * ROW_GROUP + dr
                pltpu.make_async_copy(moved_any.at[k], planes.at[k], plane_sems.at[k]).wait()
        for dr in range(ROW_GROUP):
            r = c * ROW_GROUP + dr
            for level in range(levels):
                k = level * rows + r
                exponent = jnp.dot(rate_ref[level], factor[r], preferred_element_type=F32)
                planes[k] = planes[k] * pl.reciprocal(1.0 + softplus(exponent), approx=False)
        for dr in range(ROW_GROUP):
            for level in range(levels):
                k = level * rows + c * ROW_GROUP + dr
                pltpu.make_async_copy(
                    planes.at[k, pl.ds(0, species), :], out_any.at[:, k, 0, :], out_sems.at[k]
                ).start()
        return carry

    lax.fori_loop(0, rows // ROW_GROUP, some_rows, 0)
    for fl in range(levfields):
        for r in range(0, rows, 8):
            tile_ref[fl, pl.ds(r, 8), :] = total[pl.ds(r * levfields + fl, 8, stride=levfields), :]
    finish(fetch([tile_ref], [tile_any], in_sems))
    for k in range(count):
        pltpu.make_async_copy(
            planes.at[k, pl.ds(0, species), :], out_any.at[:, k, 0, :], out_sems.at[k]
        ).wait()


def chemistry(labels, second, met, light, rate, moved, levels, species):
    owners, _, cells = second.shape
    count, padded, _ = moved.shape
    rows = count // levels
    levfields = second.shape[1] // CAP + 12
    depth = rate.shape[2]
    tile = jax.ShapeDtypeStruct((levfields, rows, cells), F32)
    return pl.pallas_call(
        functools.partial(chemistry_kernel, levels),
        out_shape=(jax.ShapeDtypeStruct((species, count, 1, cells), F32), tile),
        in_specs=here(6),
        out_specs=tuple(here(2)),
        scratch_shapes=[
            pltpu.SMEM(labels.shape, jnp.int32),
            *buffers([second, met, light, rate, moved, tile]),
            pltpu.VMEM(((rows + 1) * levfields, cells), F32),
            pltpu.VMEM((rows, depth, cells), BF16),
            pltpu.SemaphoreType.DMA((5,)), pltpu.SemaphoreType.DMA((count,)), pltpu.SemaphoreType.DMA((count,)),
        ],
        compiler_params=params(BIG),
        cost_estimate=pl.CostEstimate(
            flops=20 * moved.size, bytes_accessed=8 * moved.size, transcendentals=3 * moved.size
        ),
        name="chemistry",
    )(labels, second, met, light, rate, moved)


def rate_factors(rate_coef, photo_coef, levels, padded):
    species, fields = rate_coef.shape
    same = jnp.eye(levels, dtype=F32)
    by_field = rate_coef[None, :, :, None] * same[:, None, None, :]
    by_light = photo_coef[None, :, None] * same[:, None, :]
    table = jnp.concatenate([by_field.reshape(levels, species, fields * levels), by_light], axis=2)
    table = jnp.pad(table, ((0, 0), (0, padded - species), (0, 64 - table.shape[2])))
    high = lax.reduce_precision(table, 8, 7)
    rest = (table - high).astype(BF16)
    high = high.astype(BF16)
    return jnp.concatenate([high, high, rest], axis=2)


def shift(x, axis, by):
    count = lax.axis_size(axis)
    return lax.ppermute(x, axis, [(i, (i + by) % count) for i in range(count)])


def local(met_src, intersection_weights, block_dest, block_row, tracers, rate_coef, photo_coef):
    owners = lax.axis_size("face") * lax.axis_size("tile")
    species, levels, rows, cells = tracers.shape
    padded = -(-species // HALF) * HALF
    tracer_planes = tracers.reshape(species, levels * rows, 1, cells)

    first, second, top, bottom = regrid(
        block_dest, block_row, met_src, intersection_weights, tracer_planes, owners, padded, levels, rows
    )
    first = lax.all_to_all(first, ("face", "tile"), split_axis=0, concat_axis=0, tiled=True)
    below = shift(bottom, "face", 1)
    above = shift(top, "face", -1)
    right, left = columns(tracer_planes, padded, levels)

    met, courant, clast, czero, light, labels = first_fields(first, levels, rows)
    second, clast, czero, right, below, above = lax.optimization_barrier(
        (second, clast, czero, right, below, above)
    )
    second = lax.all_to_all(second, ("face", "tile"), split_axis=0, concat_axis=0, tiled=True)
    cbelow = shift(clast, "face", 1)
    cabove = shift(czero, "face", -1)
    right_send, left_send, cright = edges(below, above, right, left, courant, cbelow, cabove)
    west = shift(right_send, "tile", 1)
    east = shift(left_send, "tile", -1)
    moved = advect(tracer_planes, below, above, right, left, west, east, courant, cbelow, cabove, cright)
    rate = rate_factors(rate_coef, photo_coef, levels, padded)
    out, met_tile = chemistry(labels, second, met, light, rate, moved, levels, species)
    fields = rate_coef.shape[1]
    return met_tile.reshape(fields, levels, rows, cells), out.reshape(species, levels, rows, cells)


def solution(mesh):
    return jax.shard_map(
        local,
        mesh=mesh,
        in_specs=(
            P(("face", "tile"), None, None),
            P(("face", "tile"), None, None),
            P(("face", "tile")),
            P(("face", "tile")),
            P(None, None, "face", "tile"),
            P(),
            P(),
        ),
        out_specs=(P(None, None, "face", "tile"), P(None, None, "face", "tile")),
        check_vma=False,
    )
```

time: 166 us -> 73.6 us (0.44)
  other arithmetic: 56.9 us -> 0.6 us
  Pallas kernels: 0 us -> 36.7 us
  local copies, waits for them, and re-layouts: 33.9 us -> 0.27 us
  matrix products: 26.9 us -> 0 us
  waiting for transfers between devices: 23.1 us -> 14.7 us
  starting transfers between devices: 23 us -> 20.3 us
    pallas_call x0 -> x6, Pallas kernels: none -> 36.7 us  [the longest x1 13.3 us: advect(): pl.pallas_call(functools.partial(advect_kernel, levels), out_shape=jax.Sh...]
    add x5 -> x0, other arithmetic: 28.9 us -> none  [the longest x2 17.1 us: local(): jnp.maximum(wind_x[:, :-1, 1:-1], 0.0) * amount[:, :, :-1, 1:-1]]
    dot_general x5 -> x0, matrix products: 26.9 us -> none  [the longest x1 22.5 us: local(): jnp.einsum('sf,flxy->slxy', rate_coef, met_tile, precision=lax.Precision....]
    unnamed x20 -> x4, local copies, waits for them, and re-layouts: 23.6 us -> 0.01 us
    sub x1 -> x0, other arithmetic: 17.9 us -> none  [local(): amount[:, :, 1:-1, 1:-1] - (flux_x[:, :, 1:, :] - flux_x[:, :, :-1, :])]
    ppermute x8 -> x6, waiting for transfers between devices: 19.6 us -> 9.59 us  [shift(): return lax.ppermute(x, axis, [(i, (i + by) % count) for i in range(count)])]
    concatenate x3 -> x2, other arithmetic: 6.63 us -> 0.31 us  [the longest x1 0.26 us: rate_factors(): return jnp.concatenate([high, high, rest], axis=2)]
    slice x2 -> x0, local copies, waits for them, and re-layouts: 4.53 us -> none  [with_halo(): lax.slice_in_dim(block, block.shape[dim] - width, None, axis=dim)]
  transfers between devices with their start and end apart: 10 -> 8, of which waited for: 5 -> 4; matrix products, arithmetic and copies ran while one was open for 19% -> 1% of each run, Pallas kernels for 0% -> 30%
where the time goes in v1:
time: 73.6 us; the launch traced here: 73.3 us
  Pallas kernels  36.7 us (50%)
  starting transfers between devices  20.3 us (28%)
  waiting for transfers between devices  14.7 us (20%)
  between operations  0.8 us (1%)
    pallas_call x1, Pallas kernels, advect(): pl.pallas_call(functools.partial(advect_kernel, levels), out_shape=jax.Sh...  13.3 us
    ppermute x6, waiting for transfers between devices, shift(): return lax.ppermute(x, axis, [(i, (i + by) % count) for i in range(count)])  9.59 us
    pallas_call x1, Pallas kernels, chemistry(): pl.pallas_call(functools.partial(chemistry_kernel, levels), out_shape=(ja...  9.02 us
    ppermute x6, starting transfers between devices, shift(): return lax.ppermute(x, axis, [(i, (i + by) % count) for i in range(count)])  8.87 us
    all_to_all x1, starting transfers between devices, local(): lax.all_to_all(first, ('face', 'tile'), split_axis=0, concat_axis=0, tile...  6.57 us
    pallas_call x1, Pallas kernels, columns(): pl.pallas_call(functools.partial(column_kernel, levels), out_shape=(side,...  5.52 us
    pallas_call x1, Pallas kernels, regrid(): pl.pallas_call(functools.partial(regrid_kernel, rows), out_shape=(first,...  5.38 us
    all_to_all x1, waiting for transfers between devices, local(): lax.all_to_all(first, ('face', 'tile'), split_axis=0, concat_axis=0, tile...  5.11 us
  transfers between devices with their start and end apart: 8, of which 4 were waited for; matrix products, arithmetic and copies ran while one was open for 1% of the time, Pallas kernels for 30%

profile of v1, /device:TPU:0, one launch (start us, length us, event | category | flops | bytes accessed | tf_op | source)
XLA Modules:
  0.0 73.3 jit_solution(3194786076078937910)
XLA Ops:
  0.6 0.0 copy-start
  0.6 0.0 copy-start.1
  0.7 5.4 %regrid.1 = (bf16[32,32,128]{2,1,0:T(8,128)(2,1)}, bf16[32,72,128]{2,1,0:T(8,128)(2,1)}, bf16[2,4,256,128]{3,2,1,0:T(8,128)(2,1)}, bf16[2,4,256,128]{3,2,1,0:T(8,128)(2,1)}) custom-call(s32[64]{0:T(128)} %dest_any.1, s32[64]{0:T(128)} %row_any.1, bf16[64,48,128]{2,1,0:T(8,128)(2,1)} %src_any.1, bf16[64,128,128]{2,1,0:T(8,128)(2,1)} %weight_any.1, ...), custom_call_target="tpu_custom_call" | custom-call | flops 100663296 | bytes 6291456 | tf_op jit(solution)/shard_map/regrid/pallas_call | solution.py:127
  6.0 0.5 collective-permute-start
  6.5 2.0 %collective-permute-start.1 = (bf16[2,4,256,128]{3,2,1,0:T(8,128)(2,1)}, bf16[2,4,256,128]{3,2,1,0:T(8,128)(2,1)S(1)}, u32[]{:S(2)}, u32[]{:S(2)}) collective-permute-start(bf16[2,4,256,128]{3,2,1,0:T(8,128)(2,1)} %get-tuple-element.32), channel_id=1, source_target_pairs={{0,24},{8,0},{16,8},{24,16},{1,25},{9,1},{17,9},{25,17},{2,26},{10... | collective-permute-start | bytes 1572872 | tf_op jit(solution)/shard_map/ppermute | solution.py:689
  8.6 6.6 %all-to-all-start = ((bf16[32,32,128]{2,1,0:T(8,128)(2,1)}), bf16[32,32,128]{2,1,0:T(8,128)(2,1)S(1)}, u32[]{:S(2)}, u32[]{:S(2)}) async-start(bf16[32,32,128]{2,1,0:T(8,128)(2,1)} %get-tuple-element.25), calls=%async_computation | async-start | bytes 524288 | tf_op jit(solution)/shard_map/all_to_all | solution.py:701
  15.1 5.5 %columns.1 = (bf16[256,128]{1,0:T(8,128)(2,1)S(1)}, bf16[256,128]{1,0:T(8,128)(2,1)S(1)}) custom-call(f32[250,64,1,128]{3,2,1,0:T(1,128)} %bitcast.7), custom_call_target="tpu_custom_call" | custom-call | flops 24576000 | bytes 8192000 | tf_op jit(solution)/shard_map/columns/pallas_call | solution.py:193
  20.7 5.1 %all-to-all-done.first_any = bf16[32,32,128]{2,1,0:T(8,128)(2,1)S(1)} async-done(((bf16[32,32,128]{2,1,0:T(8,128)(2,1)}), bf16[32,32,128]{2,1,0:T(8,128)(2,1)S(1)}, u32[]{:S(2)}, u32[]{:S(2)}) %all-to-all-start) | async-done | bytes 262176 | tf_op jit(solution)/shard_map/all_to_all | solution.py:701
  25.8 2.3 %first_fields.1 = (f32[16,16,128]{2,1,0:T(8,128)S(1)}, f32[16,8,128]{2,1,0:T(8,128)S(1)}, f32[2,8,128]{2,1,0:T(8,128)S(1)}, f32[1,8,128]{2,1,0:T(8,128)S(1)}, f32[16,8,128]{2,1,0:T(8,128)S(1)}, /*index=5*/s32[64]{0:T(128)S(1)}) custom-call(bf16[32,32,128]{2,1,0:T(8,128)(2,1)S(1)} %all-to-all-done.first_any), custom_call_target="tpu_custom_call" | custom-call | flops 1048576 | bytes 2097152 | tf_op jit(solution)/shard_map/first_fields/pallas_call | solution.py:276
  28.1 0.0 collective-permute-done.below_any
  28.1 0.0 collective-permute-done.1.above_any
  28.2 4.8 %all-to-all-start.1 = ((bf16[32,72,128]{2,1,0:T(8,128)(2,1)}), bf16[32,72,128]{2,1,0:T(8,128)(2,1)S(1)}, u32[]{:S(2)}, u32[]{:S(2)}) async-start(bf16[32,72,128]{2,1,0:T(8,128)(2,1)} %get-tuple-element.33), calls=%async_computation.1 | async-start | bytes 1179648 | tf_op jit(solution)/shard_map/all_to_all | solution.py:710
  33.0 0.0 copy-done
  33.1 0.0 copy-done.1
  33.1 0.1 broadcast_multiply_fusion.1
  33.2 0.1 broadcast_multiply_fusion
  33.3 1.6 %collective-permute-start.3 = (f32[1,8,128]{2,1,0:T(8,128)S(1)}, f32[1,8,128]{2,1,0:T(8,128)S(1)}, u32[]{:S(2)}, u32[]{:S(2)}) collective-permute-start(f32[1,8,128]{2,1,0:T(8,128)S(1)} %get-tuple-element.42), channel_id=1, source_target_pairs={{0,24},{8,0},{16,8},{24,16},{1,25},{9,1},{17,9},{25,17},{2,26},{10... | collective-permute-start | bytes 12296 | tf_op jit(solution)/shard_map/ppermute | solution.py:689
  34.9 0.0 collective-permute-start.2
  34.9 0.1 pad_maximum_fusion.1
  34.9 0.2 copy.13
  35.2 1.0 %collective-permute-done.3.cabove_any = f32[1,8,128]{2,1,0:T(8,128)S(1)} collective-permute-done((f32[1,8,128]{2,1,0:T(8,128)S(1)}, f32[1,8,128]{2,1,0:T(8,128)S(1)}, u32[]{:S(2)}, u32[]{:S(2)}) %collective-permute-start.3) | collective-permute-done | bytes 4128 | tf_op jit(solution)/shard_map/ppermute | solution.py:689
  36.2 1.7 %collective-permute-done.2.cbelow_any = f32[2,8,128]{2,1,0:T(8,128)S(1)} collective-permute-done((f32[2,8,128]{2,1,0:T(8,128)S(1)}, f32[2,8,128]{2,1,0:T(8,128)S(1)}, u32[]{:S(2)}, u32[]{:S(2)}) %collective-permute-start.2) | collective-permute-done | bytes 8224 | tf_op jit(solution)/shard_map/ppermute | solution.py:689
  37.9 1.1 %edges.1 = (bf16[528,128]{1,0:T(8,128)(2,1)S(1)}, bf16[528,128]{1,0:T(8,128)(2,1)S(1)}, f32[8,128]{1,0:T(8,128)S(1)}) custom-call(bf16[2,4,256,128]{3,2,1,0:T(8,128)(2,1)S(1)} %collective-permute-done.below_any, bf16[2,4,256,128]{3,2,1,0:T(8,128)(2,1)S(1)} %collective-permute-done.1.above_any, bf16[256,128]{1,0:T(8,128)(2,1)S(1)} %get-tuple-element.38.right_any, ...), custom_call_target="tpu_custom_call" | custom-call | flops 262144 | bytes 2097152 | tf_op jit(solution)/shard_map/edges/pallas_call | solution.py:342
  39.1 1.6 %collective-permute-start.4 = (bf16[528,128]{1,0:T(8,128)(2,1)S(1)}, bf16[528,128]{1,0:T(8,128)(2,1)S(1)}, u32[]{:S(2)}, u32[]{:S(2)}) collective-permute-start(bf16[528,128]{1,0:T(8,128)(2,1)S(1)} %get-tuple-element.43), channel_id=1, source_target_pairs={{0,1},{1,2},{2,3},{3,4},{4,5},{5,6},{6,7},{7,0},{8,9},{9,10},{10,1... | collective-permute-start | bytes 405512 | tf_op jit(solution)/shard_map/ppermute | solution.py:689
  40.7 3.2 %collective-permute-start.5 = (bf16[528,128]{1,0:T(8,128)(2,1)S(1)}, bf16[528,128]{1,0:T(8,128)(2,1)S(1)}, u32[]{:S(2)}, u32[]{:S(2)}) collective-permute-start(bf16[528,128]{1,0:T(8,128)(2,1)S(1)} %get-tuple-element.44), channel_id=1, source_target_pairs={{0,7},{1,0},{2,1},{3,2},{4,3},{5,4},{6,5},{7,6},{8,15},{9,8},{10,9... | collective-permute-start | bytes 405512 | tf_op jit(solution)/shard_map/ppermute | solution.py:689
  43.9 0.1 reduce-precision_convert_fusion
  44.0 0.3 pad_maximum_fusion.rate_any
  44.2 6.8 %collective-permute-done.4.west_any = bf16[528,128]{1,0:T(8,128)(2,1)S(1)} collective-permute-done((bf16[528,128]{1,0:T(8,128)(2,1)S(1)}, bf16[528,128]{1,0:T(8,128)(2,1)S(1)}, u32[]{:S(2)}, u32[]{:S(2)}) %collective-permute-start.4) | collective-permute-done | bytes 135200 | tf_op jit(solution)/shard_map/ppermute | solution.py:689
  51.0 0.0 collective-permute-done.5.east_any
  51.0 13.3 %advect.1.moved_any = f32[64,256,128]{2,1,0:T(8,128)} custom-call(f32[250,64,1,128]{3,2,1,0:T(1,128)} %bitcast.8, bf16[2,4,256,128]{3,2,1,0:T(8,128)(2,1)S(1)} %collective-permute-done.below_any, bf16[2,4,256,128]{3,2,1,0:T(8,128)(2,1)S(1)} %collective-permute-done.1.above_any, bf16[256,128]{1,0:T(8,128)(2,1)S(1)} %get-tuple-element.38.right_any, ...), custom_call_target="tpu_custom_call" | custom-call | flops 81920000 | bytes 16384000 | tf_op jit(solution)/shard_map/advect/pallas_call | solution.py:547
  64.3 0.0 all-to-all-done.1.second_any
  64.3 9.0 %chemistry.1 = (f32[250,64,1,128]{3,2,1,0:T(1,128)}, f32[48,16,128]{2,1,0:T(8,128)}) custom-call(s32[64]{0:T(128)S(1)} %get-tuple-element.26.label_any, bf16[32,72,128]{2,1,0:T(8,128)(2,1)S(1)} %all-to-all-done.1.second_any, f32[16,16,128]{2,1,0:T(8,128)S(1)} %get-tuple-element.34.met_any, f32[16,8,128]{2,1,0:T(8,128)S(1)} %get-tuple-element.35.light_any, ...), custom_call_target="tpu_custom_call" | custom-call | flops 41943040 | bytes 16777216 | tf_op jit(solution)/shard_map/chemistry/pallas_call | solution.py:654
  (4 shorter events, 0.0 us)
Async XLA Ops:
  0.6 32.4 %copy-start = (f32[250,12]{0,1:T(8,128)S(1)}, f32[250,12]{0,1:T(8,128)}, u32[]{:S(2)}) copy-start(f32[250,12]{0,1:T(8,128)} %param.12) | copy-start | bytes 36004
  0.6 32.4 %copy-start.1 = (f32[250]{0:T(256)S(1)}, f32[250]{0:T(256)}, u32[]{:S(2)}) copy-start(f32[250]{0:T(256)} %param.13) | copy-start | bytes 3004
  6.0 22.1 %collective-permute-start = (bf16[2,4,256,128]{3,2,1,0:T(8,128)(2,1)}, bf16[2,4,256,128]{3,2,1,0:T(8,128)(2,1)S(1)}, u32[]{:S(2)}, u32[]{:S(2)}) collective-permute-start(bf16[2,4,256,128]{3,2,1,0:T(8,128)(2,1)} %get-tuple-element.31), channel_id=1, source_target_pairs={{0,8},{8,16},{16,24},{24,0},{1,9},{9,17},{17,25},{25,1},{2,10},{10... | collective-permute-start | bytes 1572872 | tf_op jit(solution)/shard_map/ppermute | solution.py:689
  6.5 21.6 %collective-permute-start.1 = (bf16[2,4,256,128]{3,2,1,0:T(8,128)(2,1)}, bf16[2,4,256,128]{3,2,1,0:T(8,128)(2,1)S(1)}, u32[]{:S(2)}, u32[]{:S(2)}) collective-permute-start(bf16[2,4,256,128]{3,2,1,0:T(8,128)(2,1)} %get-tuple-element.32), channel_id=1, source_target_pairs={{0,24},{8,0},{16,8},{24,16},{1,25},{9,1},{17,9},{25,17},{2,26},{10... | collective-permute-start | bytes 1572872 | tf_op jit(solution)/shard_map/ppermute | solution.py:689
  8.6 17.2 %all-to-all-start = ((bf16[32,32,128]{2,1,0:T(8,128)(2,1)}), bf16[32,32,128]{2,1,0:T(8,128)(2,1)S(1)}, u32[]{:S(2)}, u32[]{:S(2)}) async-start(bf16[32,32,128]{2,1,0:T(8,128)(2,1)} %get-tuple-element.25), calls=%async_computation | async-start | bytes 524288 | tf_op jit(solution)/shard_map/all_to_all | solution.py:701
  28.2 36.1 %all-to-all-start.1 = ((bf16[32,72,128]{2,1,0:T(8,128)(2,1)}), bf16[32,72,128]{2,1,0:T(8,128)(2,1)S(1)}, u32[]{:S(2)}, u32[]{:S(2)}) async-start(bf16[32,72,128]{2,1,0:T(8,128)(2,1)} %get-tuple-element.33), calls=%async_computation.1 | async-start | bytes 1179648 | tf_op jit(solution)/shard_map/all_to_all | solution.py:710
  33.3 2.9 %collective-permute-start.3 = (f32[1,8,128]{2,1,0:T(8,128)S(1)}, f32[1,8,128]{2,1,0:T(8,128)S(1)}, u32[]{:S(2)}, u32[]{:S(2)}) collective-permute-start(f32[1,8,128]{2,1,0:T(8,128)S(1)} %get-tuple-element.42), channel_id=1, source_target_pairs={{0,24},{8,0},{16,8},{24,16},{1,25},{9,1},{17,9},{25,17},{2,26},{10... | collective-permute-start | bytes 12296 | tf_op jit(solution)/shard_map/ppermute | solution.py:689
  34.9 3.1 %collective-permute-start.2 = (f32[2,8,128]{2,1,0:T(8,128)S(1)}, f32[2,8,128]{2,1,0:T(8,128)S(1)}, u32[]{:S(2)}, u32[]{:S(2)}) collective-permute-start(f32[2,8,128]{2,1,0:T(8,128)S(1)} %get-tuple-element.41), channel_id=1, source_target_pairs={{0,8},{8,16},{16,24},{24,0},{1,9},{9,17},{17,25},{25,1},{2,10},{10... | collective-permute-start | bytes 24584 | tf_op jit(solution)/shard_map/ppermute | solution.py:689
  39.1 11.9 %collective-permute-start.4 = (bf16[528,128]{1,0:T(8,128)(2,1)S(1)}, bf16[528,128]{1,0:T(8,128)(2,1)S(1)}, u32[]{:S(2)}, u32[]{:S(2)}) collective-permute-start(bf16[528,128]{1,0:T(8,128)(2,1)S(1)} %get-tuple-element.43), channel_id=1, source_target_pairs={{0,1},{1,2},{2,3},{3,4},{4,5},{5,6},{6,7},{7,0},{8,9},{9,10},{10,1... | collective-permute-start | bytes 405512 | tf_op jit(solution)/shard_map/ppermute | solution.py:689
  40.7 10.3 %collective-permute-start.5 = (bf16[528,128]{1,0:T(8,128)(2,1)S(1)}, bf16[528,128]{1,0:T(8,128)(2,1)S(1)}, u32[]{:S(2)}, u32[]{:S(2)}) collective-permute-start(bf16[528,128]{1,0:T(8,128)(2,1)S(1)} %get-tuple-element.44), channel_id=1, source_target_pairs={{0,7},{1,0},{2,1},{3,2},{4,3},{5,4},{6,5},{7,6},{8,15},{9,8},{10,9... | collective-permute-start | bytes 405512 | tf_op jit(solution)/shard_map/ppermute | solution.py:689

commit v2 on v1

v2 whole, which is shorter than its diff:
```python
import functools

import jax
import jax.numpy as jnp
from jax import lax
from jax.experimental import pallas as pl
from jax.experimental.pallas import tpu as pltpu
from jax.sharding import PartitionSpec as P

CAP = 2
F32 = jnp.float32
BF16 = jnp.bfloat16
HALF = 256
COL = 50
BIG = 50
ADV = 50
BIGGEST = 60
MIB = 1024 * 1024
SMEM = pltpu.MemorySpace.SMEM
VMEM = pltpu.MemorySpace.VMEM


def here(count):
    return [pl.BlockSpec(memory_space=pl.ANY)] * count


def params(mib):
    return pltpu.CompilerParams(vmem_limit_bytes=mib * MIB)


def buffers(arrays):
    return [pltpu.VMEM(x.shape, x.dtype) for x in arrays]


def fetch(sources, targets, sems):
    copies = [pltpu.make_async_copy(s, t, sems.at[i]) for i, (s, t) in enumerate(zip(sources, targets))]
    for copy in copies:
        copy.start()
    return copies


def finish(copies):
    for copy in copies:
        copy.wait()


def lanes(shape):
    return lax.broadcasted_iota(jnp.int32, shape, len(shape) - 1)


def sublanes(shape):
    return lax.broadcasted_iota(jnp.int32, shape, len(shape) - 2)


def turn(x, shift):
    count = x.shape[-1]
    shift = shift % count
    return x if shift == 0 else pltpu.roll(x, shift, x.ndim - 1)


def regrid_kernel(n_tile, rows, dest_any, row_any, src_any, weight_any, out_any,
                  dest_ref, row_ref, src_ref, weight_ref, out_ref, line_ref, column_ref, index_ref, count_ref, sems):
    owners = out_ref.shape[0]
    n_face = owners // n_tile
    blocks, levfields, cells = src_ref.shape
    copies = fetch([dest_any, row_any, src_any, weight_any], [dest_ref, row_ref, src_ref, weight_ref], sems)

    def clear(d, carry):
        count_ref[d] = 0
        for k in range(CAP):
            index_ref[d * CAP + k] = -1
        return carry

    lax.fori_loop(0, owners, clear, 0, unroll=8)
    finish(copies[:2])

    def place(b, carry):
        d = dest_ref[b]
        k = count_ref[d]
        index_ref[d * CAP + jnp.minimum(k, CAP - 1)] = b
        count_ref[d] = k + 1
        return carry

    lax.fori_loop(0, blocks, place, 0, unroll=8)
    finish(copies[2:])
    lane = lanes((8, cells))
    pair = lane // 2
    half = cells // 2
    tail = CAP * levfields

    def product(d, carry):
        zero = jnp.zeros((8, cells), F32)
        west, east, line = zero, zero, [zero, zero, zero]
        labels = zero
        for k in range(CAP):
            b = index_ref[d * CAP + k]
            used = b >= 0
            at = jnp.maximum(b, 0)
            x = jnp.dot(src_ref[at], weight_ref[at], preferred_element_type=F32)
            x = jnp.where(used, x, 0.0).astype(BF16)
            out_ref[d, pl.ds(k * levfields, levfields), :] = x
            head = x[0:16].astype(F32)[0:8]
            row = jnp.where(used, row_ref[at], rows)
            moved = pltpu.roll(head, jnp.mod(2 * row + 6, cells), 1)
            west += jnp.where(pair == row + 2, moved, 0.0)
            east += jnp.where(pair == row + 3, moved, 0.0)
            for n, r in enumerate((rows - 1, 0, rows - 2)):
                line[n] += jnp.where(row == r, head, 0.0)
            labels = jnp.where(lane == 2 * rows + 8 + k, row.astype(F32), labels)
        column = jnp.where(lane < half, west, 0.0) + turn(east, half - 2)
        column_ref[d, 0] = column
        column_ref[d, 1] = turn(column, -2 * rows)
        column_ref[d, 2] = turn(column, 2 * rows)
        column_ref[d, 3] = labels
        for n in range(3):
            line_ref[d, n] = line[n]
        return carry

    lax.fori_loop(0, owners, product, 0, unroll=8)
    inside = lane % half
    in_rows = (inside >= 4) & (inside < 4 + 2 * rows)
    before = (inside >= 2) & (inside < 4)
    after = (inside >= 4 + 2 * rows) & (inside < 6 + 2 * rows)
    is_west = lane < half

    def surround(d, carry):
        f, t = d // n_tile, d % n_tile
        up, down = jnp.where(f == 0, n_face - 1, f - 1), jnp.where(f == n_face - 1, 0, f + 1)
        low, high = jnp.where(t == 0, n_tile - 1, t - 1), jnp.where(t == n_tile - 1, 0, t + 1)
        tile = column_ref[d, 3]
        for side, x in ((is_west, low), (~is_west, high)):
            tile += jnp.where(side & in_rows, column_ref[f * n_tile + x, 0], 0.0)
            tile += jnp.where(side & before, column_ref[up * n_tile + x, 1], 0.0)
            tile += jnp.where(side & after, column_ref[down * n_tile + x, 2], 0.0)
        parts = [tile, line_ref[up * n_tile + t, 0], line_ref[down * n_tile + t, 1], line_ref[up * n_tile + t, 2]]
        out_ref[d, pl.ds(tail, 32), :] = jnp.concatenate(parts, axis=0).astype(BF16)
        return carry

    lax.fori_loop(0, owners, surround, 0, unroll=4)
    finish(fetch([out_ref], [out_any], sems))


def regrid(block_dest, block_row, met_src, weights, n_face, n_tile, rows):
    blocks, levfields, cells = met_src.shape
    owners = n_face * n_tile
    out = jax.ShapeDtypeStruct((owners, CAP * levfields + 32, cells), BF16)
    return pl.pallas_call(
        functools.partial(regrid_kernel, n_tile, rows),
        out_shape=out,
        in_specs=here(4),
        out_specs=here(1)[0],
        scratch_shapes=[
            pltpu.SMEM(block_dest.shape, jnp.int32), pltpu.SMEM(block_row.shape, jnp.int32),
            *buffers([met_src, weights, out]),
            pltpu.VMEM((owners, 3, 8, cells), F32), pltpu.VMEM((owners, 4, 8, cells), F32),
            pltpu.SMEM((owners * CAP,), jnp.int32), pltpu.SMEM((owners,), jnp.int32),
            pltpu.SemaphoreType.DMA((4,)),
        ],
        compiler_params=params(BIGGEST),
        cost_estimate=pl.CostEstimate(
            flops=2 * blocks * levfields * cells * cells, bytes_accessed=6 * MIB, transcendentals=0
        ),
        name="regrid",
    )(block_dest, block_row, met_src, weights)


def own_lanes(padded, cells, width):
    shape = (padded, cells)
    return lanes(shape) // width == sublanes(shape) % 8


def row_kernel(rows, tracer_any, top_any, bottom_any, corner_any, border, top_ref, bottom_ref, corner_ref, sems):
    levels, padded, cells = top_ref.shape[1:]
    species = tracer_any.shape[0]
    width = 4 * levels
    sub, lane = sublanes((cells, cells)), lanes((cells, cells)) % width
    column = jnp.where(lane % 2 == 0, cells - 1, 0)
    spread_out = jnp.zeros((padded, cells), F32)
    wanted = [(level, row) for level in range(levels) for row in (0, 1, rows - 2, rows - 1)]
    finish(fetch(
        [tracer_any.at[:, level * rows + row, 0, :] for level, row in wanted],
        [border.at[i, pl.ds(0, species), :] for i in range(len(wanted))], sems,
    ))
    for i, (level, row) in enumerate(wanted):
        x = border[i].astype(BF16)
        if row < 2:
            top_ref[row, level] = x
        else:
            bottom_ref[row - rows + 2, level] = x
        if row in (0, rows - 1):
            from_row = lane // 2 == 2 * level + (1 if row == 0 else 0)
            select = jnp.where((sub == column) & from_row, 1.0, 0.0).astype(BF16)
            spread_out += jnp.dot(x, select, preferred_element_type=F32)
    packed = jnp.where(own_lanes(padded, cells, width), spread_out, 0.0)
    corner_ref[...] = jnp.sum(packed.reshape(padded // 8, 8, cells), axis=1).astype(BF16)
    finish(fetch([top_ref, bottom_ref, corner_ref], [top_any, bottom_any, corner_any], sems))


def border_rows(planes, padded, levels, rows):
    cells = planes.shape[3]
    line = jax.ShapeDtypeStruct((2, levels, padded, cells), BF16)
    corner = jax.ShapeDtypeStruct((padded // 8, cells), BF16)
    return pl.pallas_call(
        functools.partial(row_kernel, rows),
        out_shape=(line, line, corner),
        in_specs=here(1),
        out_specs=tuple(here(3)),
        scratch_shapes=[
            pltpu.VMEM((4 * levels, padded, cells), F32), *buffers([line, line, corner]),
            pltpu.SemaphoreType.DMA((4 * levels,)),
        ],
        compiler_params=params(BIG),
        cost_estimate=pl.CostEstimate(flops=planes.size, bytes_accessed=planes.size, transcendentals=0),
        name="border_rows",
    )(planes)


def load_planes(source, target, sems):
    species = source.shape[0]
    copies = []
    for k in range(source.shape[1]):
        copy = pltpu.make_async_copy(source.at[:, k, 0, :], target.at[k, pl.ds(0, species), :], sems.at[k])
        copy.start()
        copies.append(copy)
    return copies


def column_kernel(levels, tracer_any, planes_any, right_ref, left_ref, planes, total, picker, sems, out_sems):
    count, padded, cells = planes.shape
    rows = count // levels
    load_planes(tracer_any, planes, sems)
    total[...] = jnp.zeros_like(total)
    picker[...] = jnp.zeros_like(picker)
    sub, lane = sublanes((16, 2 * cells)), lanes((16, 2 * cells))

    def one_level(level, carry):
        for row in range(rows):
            pltpu.make_async_copy(
                tracer_any.at[:, level * rows + row, 0, :],
                planes.at[level * rows + row, pl.ds(0, tracer_any.shape[0]), :],
                sems.at[level * rows + row],
            ).wait()
        part = pl.ds(level * rows, rows)
        pltpu.make_async_copy(planes.at[part], planes_any.at[part], out_sems.at[level]).start()
        for row in range(0, rows, 2):
            pair = []
            for h in range(2):
                k = level * rows + row + h
                pair.append(planes[k].astype(BF16))
                low = (sub < 2) & (lane == cells + 2 * k + sub)
                high = (sub >= 14) & (lane == 2 * k + sub - 14)
                picker[row // 2, pl.ds(h * cells, 16), :] = jnp.where(low, 1.0, 0.0).astype(BF16)
                picker[row // 2, pl.ds((h + 1) * cells - 16, 16), :] = jnp.where(high, 1.0, 0.0).astype(BF16)
            both = jnp.concatenate(pair, axis=1)
            total[...] += jnp.dot(both, picker[row // 2], preferred_element_type=F32)
        return carry

    lax.fori_loop(0, levels, one_level, 0)
    for level in range(levels):
        part = pl.ds(level * rows, rows)
        pltpu.make_async_copy(planes.at[part], planes_any.at[part], out_sems.at[level]).wait()
    right_ref[...] = total[:, 0:cells].astype(BF16)
    left_ref[...] = total[:, cells:].astype(BF16)


def columns(planes, padded, levels):
    _, count, _, cells = planes.shape
    side = jax.ShapeDtypeStruct((padded, cells), BF16)
    return pl.pallas_call(
        functools.partial(column_kernel, levels),
        out_shape=(
            jax.ShapeDtypeStruct((count, padded, cells), F32), side, side,
        ),
        in_specs=here(1),
        out_specs=(*here(1), *[pl.BlockSpec(memory_space=VMEM)] * 2),
        scratch_shapes=[
            pltpu.VMEM((count, padded, cells), F32),
            pltpu.VMEM((padded, 2 * cells), F32), pltpu.VMEM((count // levels // 2, 2 * cells, 2 * cells), BF16),
            pltpu.SemaphoreType.DMA((count,)), pltpu.SemaphoreType.DMA((levels,)),
        ],
        compiler_params=params(COL),
        cost_estimate=pl.CostEstimate(flops=12 * planes.size, bytes_accessed=4 * planes.size, transcendentals=0),
        name="columns",
    )(planes)


def softplus(x):
    return jnp.maximum(x, jnp.log(1.0 + jnp.exp(jnp.minimum(x, 60.0))))


def five_weights(face_x, face_x_low, face_y, face_y_low):
    up = -jnp.minimum(face_x, 0.0)
    down = jnp.maximum(face_x_low, 0.0)
    right = -jnp.minimum(face_y, 0.0)
    left = jnp.maximum(face_y_low, 0.0)
    stay = (
        1.0
        - (jnp.maximum(face_x, 0.0) - jnp.minimum(face_x_low, 0.0))
        - (jnp.maximum(face_y, 0.0) - jnp.minimum(face_y_low, 0.0))
    )
    return stay, up, down, left, right


def spread(x, level, count):
    return jnp.broadcast_to(x[level : level + 1], (count, x.shape[1]))


def make_weights(levels, line, west, east, inner, side, edge):
    rows = len(line) - 3
    fields, cells = line[0].shape
    lane = lanes((fields, cells))
    own_right = jnp.zeros((fields, cells), F32)
    for i in range(2, rows + 2):
        own_right = jnp.where(lane // 2 == i, turn(line[i], 2 * i - (cells - 2)), own_right)
    for i in range(1, rows + 3):
        now, low = line[i], line[i - 1]
        face_y_low = jnp.where(lane == 0, turn(west, -(2 * i + 1)), turn(now, 1))[levels:]
        five = five_weights(now[:levels], low[:levels], now[levels:], face_y_low)
        for level in range(levels):
            for c in range(3):
                inner[level, i - 1, c] = spread(five[c], level, 8)
            for c in range(2):
                side[level, i - 1, c] = spread(five[3 + c], level, 16).astype(BF16)
    odd = lane % 2 == 1
    middle = jnp.where(odd, west, east)
    lower = turn(middle, 2)
    y_low = jnp.where(odd, turn(west, 1), turn(own_right, -1))
    stay, up, down, left, right = five_weights(
        middle[:levels], lower[:levels], middle[levels:], y_low[levels:]
    )
    odd = odd[:levels]
    outer_w = jnp.where(odd, left, right)
    inner_w = jnp.where(odd, right, left)
    lane8 = lanes((8, cells))
    span = cells // levels
    for c, x in enumerate((stay, up, down, outer_w, inner_w)):
        out = jnp.zeros((8, cells), F32)
        for level in range(levels):
            out = jnp.where(lane8 // span == level, turn(spread(x, level, 8), level * span - 4), out)
        edge[c] = out


def place_corners(levels, came, corner_ref):
    padded, cells = corner_ref.shape
    width = 4 * levels
    span = cells // levels
    mine = own_lanes(padded, cells, width)
    parts, picks = [], []
    sub, lane = sublanes((cells, cells)) % width, lanes((cells, cells))
    for n, x in enumerate(came):
        x = jnp.broadcast_to(x.astype(F32)[:, None, :], (padded // 8, 8, cells))
        parts.append(jnp.where(mine, x.reshape(padded, cells), 0.0).astype(BF16))
        target = sub // 4 * span + (1, 0, span - 1, span - 2)[n]
        picks.append(jnp.where((sub % 4 == n) & (lane == target), 1.0, 0.0).astype(BF16))
    both = jnp.dot(
        jnp.concatenate(parts, axis=1), jnp.concatenate(picks, axis=0), preferred_element_type=F32
    )
    corner_ref[...] = both.astype(BF16)


def side_columns(rows, levels, right_ref, left_ref, west_ref, east_ref, edge, mid_ref, corner_ref, next_ref):
    padded, cells = right_ref.shape
    span = cells // levels
    lane = lanes((16, cells))
    odd = lane % 2 == 1
    row_of = (lane % span) // 2

    def group(g, carry):
        part = pl.ds(pl.multiple_of(g * 16, 16), 16)
        lo, hi = west_ref[part, :].astype(F32), east_ref[part, :].astype(F32)
        own_r, own_l = right_ref[part, :].astype(F32), left_ref[part, :].astype(F32)
        corner = corner_ref[part, :].astype(F32)
        weights = [jnp.concatenate([edge[c]] * 2, axis=0) for c in range(5)]
        mid = jnp.where(odd, lo, hi)
        outside = jnp.where(odd, turn(lo, 1), turn(hi, -1))
        inside = jnp.where(odd, turn(own_l, 1), turn(own_r, -1))
        above = jnp.where(row_of == rows - 1, corner, turn(mid, -2))
        below = jnp.where(row_of == 0, corner, turn(mid, 2))
        mid_ref[part, :] = mid.astype(BF16)
        after = (
            weights[0] * mid + weights[1] * above + weights[2] * below
            + weights[3] * outside + weights[4] * inside
        )
        next_ref[part, :] = after.astype(BF16)
        return carry

    lax.fori_loop(0, padded // 16, group, 0, unroll=2)


def gather_fields(came_ref, label_v, label_s, total, beside, sem):
    owners, _, cells = came_ref.shape
    levfields = (came_ref.shape[1] - 32) // CAP
    rows = total.shape[0] // levfields - 1
    tail = CAP * levfields

    def read(d, sums):
        x = came_ref[d, pl.ds(tail, 32), :].astype(F32)
        label_v[pl.ds(d, 1), :] = x[0:1].astype(jnp.int32)
        return sums + x

    beside[...] = lax.fori_loop(0, owners, read, jnp.zeros((32, cells), F32), unroll=4)
    copies = fetch([label_v], [label_s], sem)
    total[...] = jnp.zeros_like(total)
    finish(copies)

    def add(d, carry):
        for k in range(CAP):
            at = pl.multiple_of(label_s[d, 2 * rows + 8 + k] * levfields, 8)
            total[pl.ds(at, levfields), :] += came_ref[d, pl.ds(k * levfields, levfields), :].astype(F32)
        return carry

    lax.fori_loop(0, owners, add, 0, unroll=4)


def light_of(levels, optical):
    depth = softplus(optical)
    parts, running = [], jnp.zeros((1, depth.shape[1]), F32)
    for level in range(levels):
        running = running + depth[level : level + 1]
        parts.append(jnp.exp(-running))
    return jnp.concatenate(parts, axis=0)


def advect_kernel(
    levels, planes_any, below_any, above_any, right_any, left_any, west_any, east_any,
    came_any, rate_any, around_any, out_any, tile_any,
    planes, below_ref, above_ref, right_ref, left_ref, west_ref, east_ref,
    came_ref, rate_ref,
    tile_ref, total, factor, label_v, label_s, ghost,
    inner, side, edge, mid_ref, corner_ref, next_ref, matrix, low_mask, high_mask, once, once16,
    plane_sems, in_sems, out_sems,
):
    levfields, rows, cells = tile_ref.shape
    padded = planes.shape[1]
    species = out_any.shape[0]
    span = cells // levels
    small = fetch(
        [came_any, rate_any, west_any, east_any, right_any, left_any, below_any, above_any],
        [came_ref, rate_ref, west_ref, east_ref, right_ref, left_ref, below_ref, above_ref], in_sems,
    )
    parts = [pl.ds(level * rows, rows) for level in range(levels)]
    fetch([planes_any.at[p] for p in parts], [planes.at[p] for p in parts], plane_sems)
    sub, lane = sublanes((cells, cells)), lanes((cells, cells))
    low_mask[...] = jnp.where(sub == lane - 1, 1.0, 0.0).astype(BF16)
    high_mask[...] = jnp.where(sub == lane + 1, 1.0, 0.0).astype(BF16)
    finish(small[:1])
    gather_fields(came_ref, label_v, label_s, total, ghost, in_sems)
    for fl in range(levfields):
        for r in range(0, rows, 8):
            tile_ref[fl, pl.ds(r, 8), :] = total[pl.ds(r * levfields + fl, 8, stride=levfields), :]
    tile_copy = fetch([tile_ref], [tile_any], in_sems)
    fields = 2 * levels
    ghosts = 0.3 * jnp.tanh(ghost[...])
    line = [ghosts[24:32], ghosts[8:16]]
    for r in range(rows):
        line.append(0.3 * jnp.tanh(total[pl.ds(r * levfields, fields), :]))
        x = total[pl.ds(r * levfields, levfields), :]
        light = light_of(levels, x[fields : fields + levels])
        x = jnp.concatenate([x, light, jnp.zeros((16 - levels, cells), F32)], axis=0)
        high = x.astype(BF16)
        rest = (x - high.astype(F32)).astype(BF16)
        factor[r] = jnp.concatenate([high, rest, high], axis=0)
    line.append(ghosts[16:24])
    make_weights(levels, line, ghosts[0:8], turn(ghosts[0:8], cells // 2), inner, side, edge)
    finish(small[1:])
    packed = padded // 8
    place_corners(levels, [
        ref[pl.ds(padded + n * packed, packed), :] for n in range(2) for ref in (west_ref, east_ref)
    ], corner_ref)
    side_columns(rows, levels, right_ref, left_ref, west_ref, east_ref, edge, mid_ref, corner_ref, next_ref)
    sub16, lane16 = sublanes((16, cells)), lanes((16, cells))

    def set_matrix(level, i):
        left, right = side[level, i + 1, 0], side[level, i + 1, 1]
        for t in range(cells // 16):
            at = pl.ds(16 * t, 16)
            matrix[i + 1, at, :] = low_mask[at, :] * left + high_mask[at, :] * right
        matrix[i + 1, pl.ds(cells, cells), :] = jnp.zeros((cells, cells), BF16)
        p = 2 * min(max(i, 0), rows - 1)
        tile = jnp.where(
            (sub16 == p % 16 + 1) & (lane16 == 0), left.astype(F32),
            jnp.where((sub16 == p % 16) & (lane16 == cells - 1), right.astype(F32), 0.0),
        )
        at = pl.multiple_of(cells + level * span + p // 16 * 16, 16)
        matrix[i + 1, pl.ds(at, 16), :] = tile.astype(BF16)

    def weighted(weights, x, up, down):
        count = x.shape[0] // 8
        stay, up_w, down_w = (w[None] for w in weights)
        x, up, down = (v.reshape(count, 8, cells) for v in (x, up, down))
        return (stay * x + up_w * up + down_w * down).reshape(count * 8, cells)

    def one_level(level, carry):
        part = pl.ds(level * rows, rows)
        pltpu.make_async_copy(planes_any.at[part], planes.at[part], plane_sems.at[level]).wait()
        for i in range(-1, rows + 1):
            set_matrix(level, i)

        def half(b, carry):
            part = pl.ds(pl.multiple_of(b * HALF, HALF), HALF)

            def before(i):
                if i < 0:
                    return below_ref[i + 2, level, part, :].astype(F32)
                if i >= rows:
                    return above_ref[i - rows, level, part, :].astype(F32)
                return planes[level * rows + i, part, :]

            for i in range(-1, rows + 1):
                x = before(i)
                beside = (mid_ref if 0 <= i < rows else corner_ref)[part, :]
                both = jnp.concatenate([x.astype(BF16), beside], axis=1)
                across = jnp.dot(both, matrix[i + 1], preferred_element_type=F32)
                weights = [inner[level, i + 1, c] for c in range(3)]
                x = weighted(weights, x, before(i + 1), before(i - 1)) + across
                once[i + 1] = x
                if 0 <= i < rows:
                    once16[i] = x.astype(BF16)
            for i in range(rows):
                both = jnp.concatenate([once16[i], next_ref[part, :]], axis=1)
                across = jnp.dot(both, matrix[i + 1], preferred_element_type=F32)
                weights = [inner[level, i + 1, c] for c in range(3)]
                moved = weighted(weights, once[i + 1], once[i + 2], once[i]) + across
                exponent = jnp.dot(rate_ref[level, part, :], factor[i], preferred_element_type=F32)
                planes[level * rows + i, part, :] = moved * pl.reciprocal(
                    1.0 + softplus(exponent), approx=False
                )
            return carry

        lax.fori_loop(0, padded // HALF, half, 0)
        for r in range(rows):
            k = level * rows + r
            pltpu.make_async_copy(
                planes.at[k, pl.ds(0, species), :], out_any.at[:, k, 0, :], out_sems.at[k]
            ).start()
        return carry

    lax.fori_loop(0, levels, one_level, 0)
    finish(tile_copy)
    for k in range(levels * rows):
        pltpu.make_async_copy(
            planes.at[k, pl.ds(0, species), :], out_any.at[:, k, 0, :], out_sems.at[k]
        ).wait()


def advect(planes, below, above, right, left, west, east, came, rate, around, species):
    levels, padded, cells = below.shape[1:]
    count = planes.shape[0]
    rows = count // levels
    owners = came.shape[0]
    levfields = (came.shape[1] - 32) // CAP
    tile = jax.ShapeDtypeStruct((levfields, rows, cells), F32)
    small = [below, above, right, left, west, east, came, rate]
    column = pltpu.VMEM((padded, cells), BF16)
    square = pltpu.VMEM((cells, cells), BF16)
    return pl.pallas_call(
        functools.partial(advect_kernel, levels),
        out_shape=(jax.ShapeDtypeStruct((species, count, 1, cells), F32), tile),
        in_specs=here(2 + len(small)),
        out_specs=tuple(here(2)),
        scratch_shapes=[
            pltpu.VMEM((count, padded, cells), F32),
            *buffers(small), *buffers([tile]),
            pltpu.VMEM(((rows + 1) * levfields, cells), F32),
            pltpu.VMEM((rows, rate.shape[2], cells), BF16),
            pltpu.VMEM((owners, cells), jnp.int32), pltpu.SMEM((owners, cells), jnp.int32),
            pltpu.VMEM((32, cells), F32),
            pltpu.VMEM((levels, rows + 2, 3, 8, cells), F32),
            pltpu.VMEM((levels, rows + 2, 2, 16, cells), BF16),
            pltpu.VMEM((5, 8, cells), F32),
            column, column, column,
            pltpu.VMEM((rows + 2, 2 * cells, cells), BF16),
            square, square,
            pltpu.VMEM((rows + 2, HALF, cells), F32),
            pltpu.VMEM((rows, HALF, cells), BF16),
            pltpu.SemaphoreType.DMA((levels,)), pltpu.SemaphoreType.DMA((len(small),)),
            pltpu.SemaphoreType.DMA((count,)),
        ],
        compiler_params=params(ADV),
        cost_estimate=pl.CostEstimate(
            flops=60 * planes.size, bytes_accessed=8 * planes.size, transcendentals=3 * planes.size
        ),
        name="advect",
    )(planes, *small, around)


def arrived_kernel(*refs):
    refs[-1][...] = jnp.zeros_like(refs[-1])


def arrived(arrays):
    return pl.pallas_call(
        arrived_kernel,
        out_shape=jax.ShapeDtypeStruct((8, 128), F32),
        in_specs=here(len(arrays)),
        compiler_params=params(1),
        cost_estimate=pl.CostEstimate(flops=MIB, bytes_accessed=0, transcendentals=0),
        name="arrived",
    )(*arrays)


def rate_factors(rate_coef, photo_coef, levels, padded):
    species, fields = rate_coef.shape
    same = jnp.eye(levels, dtype=F32)
    by_field = rate_coef[None, :, :, None] * same[:, None, None, :]
    by_light = photo_coef[None, :, None] * same[:, None, :]
    table = jnp.concatenate([by_field.reshape(levels, species, fields * levels), by_light], axis=2)
    table = jnp.pad(table, ((0, 0), (0, padded - species), (0, 64 - table.shape[2])))
    high = lax.reduce_precision(table, 8, 7)
    rest = (table - high).astype(BF16)
    high = high.astype(BF16)
    return jnp.concatenate([high, high, rest], axis=2)


def shift(x, axis, by):
    count = lax.axis_size(axis)
    return lax.ppermute(x, axis, [(i, (i + by) % count) for i in range(count)])


def local(met_src, intersection_weights, block_dest, block_row, tracers, rate_coef, photo_coef):
    n_face, n_tile = lax.axis_size("face"), lax.axis_size("tile")
    species, levels, rows, cells = tracers.shape
    padded = -(-species // HALF) * HALF
    tracer_planes = tracers.reshape(species, levels * rows, 1, cells)

    payload = regrid(block_dest, block_row, met_src, intersection_weights, n_face, n_tile, rows)
    payload, tracer_planes = lax.optimization_barrier((payload, tracer_planes))
    came = lax.all_to_all(payload, ("face", "tile"), split_axis=0, concat_axis=0, tiled=True)

    top, bottom, corner = border_rows(tracer_planes, padded, levels, rows)
    corner_below = shift(corner, "face", 1)
    corner_above = shift(corner, "face", -1)
    below = shift(bottom, "face", 1)
    above = shift(top, "face", -1)
    tracer_planes, top, bottom = lax.optimization_barrier((tracer_planes, top, bottom))
    planes, right, left = columns(tracer_planes, padded, levels)
    west = shift(jnp.concatenate([right, corner_below, corner_above], axis=0), "tile", 1)
    east = shift(jnp.concatenate([left, corner_below, corner_above], axis=0), "tile", -1)
    beside = arrived([west, east])
    around = arrived([below, above, beside])
    rate = rate_factors(rate_coef, photo_coef, levels, padded)
    out, met_tile = advect(planes, below, above, right, left, west, east, came, rate, around, species)
    fields = rate_coef.shape[1]
    return met_tile.reshape(fields, levels, rows, cells), out.reshape(species, levels, rows, cells)


def solution(mesh):
    return jax.shard_map(
        local,
        mesh=mesh,
        in_specs=(
            P(("face", "tile"), None, None),
            P(("face", "tile"), None, None),
            P(("face", "tile")),
            P(("face", "tile")),
            P(None, None, "face", "tile"),
            P(),
            P(),
        ),
        out_specs=(P(None, None, "face", "tile"), P(None, None, "face", "tile")),
        check_vma=False,
    )
```

time: 73.6 us -> 56.9 us (0.77)
  Pallas kernels: 36.7 us -> 30.5 us
  starting transfers between devices: 20.3 us -> 14.9 us
  waiting for transfers between devices: 14.7 us -> 9.58 us
    pallas_call x6, Pallas kernels: 36.7 us -> 30.5 us  [the longest x1 14 us: advect(): pl.pallas_call(functools.partial(advect_kernel, levels), out_shape=(jax.S...]
    all_to_all x2 -> x1, starting transfers between devices: 11.4 us -> 7.29 us  [local(): lax.all_to_all(payload, ('face', 'tile'), split_axis=0, concat_axis=0, ti...]
    all_to_all x2 -> x1, waiting for transfers between devices: 5.12 us -> 2.33 us  [local(): lax.all_to_all(payload, ('face', 'tile'), split_axis=0, concat_axis=0, ti...]
    ppermute x6, waiting for transfers between devices: 9.59 us -> 7.26 us  [shift(): return lax.ppermute(x, axis, [(i, (i + by) % count) for i in range(count)])]
    ppermute x6, starting transfers between devices: 8.87 us -> 7.64 us  [shift(): return lax.ppermute(x, axis, [(i, (i + by) % count) for i in range(count)])]
  transfers between devices with their start and end apart: 8 -> 7, of which waited for: 4 -> 3; matrix products, arithmetic and copies ran while one was open for 1% -> 2% of each run, Pallas kernels for 30% -> 20%
where the time goes in v2:
time: 56.9 us; the launch traced here: 56.7 us
  Pallas kernels  30.5 us (54%)
  starting transfers between devices  14.9 us (26%)
  waiting for transfers between devices  9.58 us (17%)
  between operations  0.79 us (1%)
  other arithmetic  0.61 us (1%)
    pallas_call x1, Pallas kernels, advect(): pl.pallas_call(functools.partial(advect_kernel, levels), out_shape=(jax.S...  14 us
    pallas_call x1, Pallas kernels, columns(): pl.pallas_call(functools.partial(column_kernel, levels), out_shape=(jax.S...  7.97 us
    ppermute x6, starting transfers between devices, shift(): return lax.ppermute(x, axis, [(i, (i + by) % count) for i in range(count)])  7.64 us
    all_to_all x1, starting transfers between devices, local(): lax.all_to_all(payload, ('face', 'tile'), split_axis=0, concat_axis=0, ti...  7.29 us
    ppermute x6, waiting for transfers between devices, shift(): return lax.ppermute(x, axis, [(i, (i + by) % count) for i in range(count)])  7.26 us
    pallas_call x1, Pallas kernels, regrid(): pl.pallas_call(functools.partial(regrid_kernel, n_tile, rows), out_shape=...  5.33 us
    pallas_call x1, Pallas kernels, border_rows(): pl.pallas_call(functools.partial(row_kernel, rows), out_shape=(line, line...  3.15 us
    all_to_all x1, waiting for transfers between devices, local(): lax.all_to_all(payload, ('face', 'tile'), split_axis=0, concat_axis=0, ti...  2.33 us
  transfers between devices with their start and end apart: 7, of which 3 were waited for; matrix products, arithmetic and copies ran while one was open for 2% of the time, Pallas kernels for 20%

profile of v2, /device:TPU:0, one launch (start us, length us, event | category | flops | bytes accessed | tf_op | source)
XLA Modules:
  0.0 56.7 jit_solution(11682912616747540562)
XLA Ops:
  0.6 0.0 copy-start
  0.6 0.0 copy-start.1
  0.7 5.3 %regrid.1 = bf16[32,128,128]{2,1,0:T(8,128)(2,1)} custom-call(s32[64]{0:T(128)} %dest_any.1, s32[64]{0:T(128)} %row_any.1, bf16[64,48,128]{2,1,0:T(8,128)(2,1)} %src_any.1, bf16[64,128,128]{2,1,0:T(8,128)(2,1)} %weight_any.1), custom_call_target="tpu_custom_call" | custom-call | flops 100663296 | bytes 6291456 | tf_op jit(solution)/shard_map/regrid/pallas_call | solution.py:147
  6.0 7.3 %all-to-all-start = ((bf16[32,128,128]{2,1,0:T(8,128)(2,1)}), bf16[32,128,128]{2,1,0:T(8,128)(2,1)S(1)}, u32[]{:S(2)}, u32[]{:S(2)}) async-start(bf16[32,128,128]{2,1,0:T(8,128)(2,1)} %regrid.1), calls=%async_computation | async-start | bytes 2097152 | tf_op jit(solution)/shard_map/all_to_all | solution.py:628
  13.3 3.1 %border_rows.1 = (bf16[2,4,256,128]{3,2,1,0:T(8,128)(2,1)}, bf16[2,4,256,128]{3,2,1,0:T(8,128)(2,1)S(1)}, bf16[32,128]{1,0:T(8,128)(2,1)S(1)}) custom-call(f32[250,64,1,128]{3,2,1,0:T(1,128)} %bitcast.6), custom_call_target="tpu_custom_call" | custom-call | flops 2048000 | bytes 2048000 | tf_op jit(solution)/shard_map/border_rows/pallas_call | solution.py:203
  16.4 1.6 %collective-permute-start.3 = (bf16[32,128]{1,0:T(8,128)(2,1)S(1)}, bf16[32,128]{1,0:T(8,128)(2,1)S(1)}, u32[]{:S(2)}, u32[]{:S(2)}) collective-permute-start(bf16[32,128]{1,0:T(8,128)(2,1)S(1)} %get-tuple-element.20), channel_id=1, source_target_pairs={{0,24},{8,0},{16,8},{24,16},{1,25},{9,1},{17,9},{25,17},{2,26},{10... | collective-permute-start | bytes 24584 | tf_op jit(solution)/shard_map/ppermute | solution.py:617
  18.0 0.0 collective-permute-start.2
  18.0 1.7 %collective-permute-start.1 = (bf16[2,4,256,128]{3,2,1,0:T(8,128)(2,1)}, bf16[2,4,256,128]{3,2,1,0:T(8,128)(2,1)S(1)}, u32[]{:S(2)}, u32[]{:S(2)}) collective-permute-start(bf16[2,4,256,128]{3,2,1,0:T(8,128)(2,1)} %get-tuple-element.14), channel_id=1, source_target_pairs={{0,24},{8,0},{16,8},{24,16},{1,25},{9,1},{17,9},{25,17},{2,26},{10... | collective-permute-start | bytes 1572872 | tf_op jit(solution)/shard_map/ppermute | solution.py:617
  19.8 0.0 collective-permute-start
  19.8 0.0 copy-done
  19.8 0.1 broadcast_multiply_fusion
  20.0 0.0 copy-done.1
  20.0 0.1 broadcast_multiply_fusion.1
  20.0 0.1 pad_maximum_fusion.1
  20.1 0.2 copy.13
  20.3 0.1 reduce-precision_convert_fusion
  20.4 8.0 %columns.1 = (f32[64,256,128]{2,1,0:T(8,128)}, bf16[256,128]{1,0:T(8,128)(2,1)S(1)}, bf16[256,128]{1,0:T(8,128)(2,1)S(1)}) custom-call(f32[250,64,1,128]{3,2,1,0:T(1,128)} %bitcast.7), custom_call_target="tpu_custom_call" | custom-call | flops 24576000 | bytes 8192000 | tf_op jit(solution)/shard_map/columns/pallas_call | solution.py:269
  28.4 0.0 collective-permute-done.3
  28.4 0.0 collective-permute-done.2
  28.5 4.3 %collective-permute-start.5 = (bf16[320,128]{1,0:T(8,128)(2,1)S(1)}, bf16[320,128]{1,0:T(8,128)(2,1)S(1)}, u32[]{:S(2)}, u32[]{:S(2)}) collective-permute-start(bf16[320,128]{1,0:T(8,128)(2,1)S(1)} %get-tuple-element.26), channel_id=1, source_target_pairs={{0,7},{1,0},{2,1},{3,2},{4,3},{5,4},{6,5},{7,6},{8,15},{9,8},{10,9... | collective-permute-start | bytes 245768 | tf_op jit(solution)/shard_map/ppermute | solution.py:617
  32.8 0.0 collective-permute-start.4
  32.8 0.3 pad_maximum_fusion.rate_any
  33.0 2.3 %collective-permute-done.5.refs_1_.east_any = bf16[320,128]{1,0:T(8,128)(2,1)S(1)} collective-permute-done((bf16[320,128]{1,0:T(8,128)(2,1)S(1)}, bf16[320,128]{1,0:T(8,128)(2,1)S(1)}, u32[]{:S(2)}, u32[]{:S(2)}) %collective-permute-start.5) | collective-permute-done | bytes 81952 | tf_op jit(solution)/shard_map/ppermute | solution.py:617
  35.3 5.0 %collective-permute-done.4.refs_0_.west_any = bf16[320,128]{1,0:T(8,128)(2,1)S(1)} collective-permute-done((bf16[320,128]{1,0:T(8,128)(2,1)S(1)}, bf16[320,128]{1,0:T(8,128)(2,1)S(1)}, u32[]{:S(2)}, u32[]{:S(2)}) %collective-permute-start.4) | collective-permute-done | bytes 81952 | tf_op jit(solution)/shard_map/ppermute | solution.py:617
  40.3 0.0 collective-permute-done.1.refs_1_.above_any
  40.3 0.0 collective-permute-done.refs_0_.below_any
  40.3 2.3 %all-to-all-done.came_any = bf16[32,128,128]{2,1,0:T(8,128)(2,1)S(1)} async-done(((bf16[32,128,128]{2,1,0:T(8,128)(2,1)}), bf16[32,128,128]{2,1,0:T(8,128)(2,1)S(1)}, u32[]{:S(2)}, u32[]{:S(2)}) %all-to-all-start) | async-done | bytes 1048608 | tf_op jit(solution)/shard_map/all_to_all | solution.py:628
  42.6 14.0 %advect.1 = (f32[250,64,1,128]{3,2,1,0:T(1,128)}, f32[48,16,128]{2,1,0:T(8,128)}) custom-call(f32[64,256,128]{2,1,0:T(8,128)} %get-tuple-element.17.planes_any, bf16[2,4,256,128]{3,2,1,0:T(8,128)(2,1)S(1)} %collective-permute-done.refs_0_.below_any, bf16[2,4,256,128]{3,2,1,0:T(8,128)(2,1)S(1)} %collective-permute-done.1.refs_1_.above_any, ...), custom_call_target="tpu_custom_call" | custom-call | flops 125829120 | bytes 16777216 | tf_op jit(solution)/shard_map/advect/pallas_call | solution.py:556
  (7 shorter events, 0.1 us)
Async XLA Ops:
  0.6 19.1 %copy-start = (f32[250,12]{0,1:T(8,128)S(1)}, f32[250,12]{0,1:T(8,128)}, u32[]{:S(2)}) copy-start(f32[250,12]{0,1:T(8,128)} %param.12) | copy-start | bytes 36004
  0.6 19.3 %copy-start.1 = (f32[250]{0:T(256)S(1)}, f32[250]{0:T(256)}, u32[]{:S(2)}) copy-start(f32[250]{0:T(256)} %param.13) | copy-start | bytes 3004
  6.0 36.6 %all-to-all-start = ((bf16[32,128,128]{2,1,0:T(8,128)(2,1)}), bf16[32,128,128]{2,1,0:T(8,128)(2,1)S(1)}, u32[]{:S(2)}, u32[]{:S(2)}) async-start(bf16[32,128,128]{2,1,0:T(8,128)(2,1)} %regrid.1), calls=%async_computation | async-start | bytes 2097152 | tf_op jit(solution)/shard_map/all_to_all | solution.py:628
  16.4 12.0 %collective-permute-start.3 = (bf16[32,128]{1,0:T(8,128)(2,1)S(1)}, bf16[32,128]{1,0:T(8,128)(2,1)S(1)}, u32[]{:S(2)}, u32[]{:S(2)}) collective-permute-start(bf16[32,128]{1,0:T(8,128)(2,1)S(1)} %get-tuple-element.20), channel_id=1, source_target_pairs={{0,24},{8,0},{16,8},{24,16},{1,25},{9,1},{17,9},{25,17},{2,26},{10... | collective-permute-start | bytes 24584 | tf_op jit(solution)/shard_map/ppermute | solution.py:617
  18.0 10.4 %collective-permute-start.2 = (bf16[32,128]{1,0:T(8,128)(2,1)S(1)}, bf16[32,128]{1,0:T(8,128)(2,1)S(1)}, u32[]{:S(2)}, u32[]{:S(2)}) collective-permute-start(bf16[32,128]{1,0:T(8,128)(2,1)S(1)} %get-tuple-element.20), channel_id=1, source_target_pairs={{0,8},{8,16},{16,24},{24,0},{1,9},{9,17},{17,25},{25,1},{2,10},{10... | collective-permute-start | bytes 24584 | tf_op jit(solution)/shard_map/ppermute | solution.py:617
  18.0 22.3 %collective-permute-start.1 = (bf16[2,4,256,128]{3,2,1,0:T(8,128)(2,1)}, bf16[2,4,256,128]{3,2,1,0:T(8,128)(2,1)S(1)}, u32[]{:S(2)}, u32[]{:S(2)}) collective-permute-start(bf16[2,4,256,128]{3,2,1,0:T(8,128)(2,1)} %get-tuple-element.14), channel_id=1, source_target_pairs={{0,24},{8,0},{16,8},{24,16},{1,25},{9,1},{17,9},{25,17},{2,26},{10... | collective-permute-start | bytes 1572872 | tf_op jit(solution)/shard_map/ppermute | solution.py:617
  19.8 20.5 %collective-permute-start = (bf16[2,4,256,128]{3,2,1,0:T(8,128)(2,1)S(1)}, bf16[2,4,256,128]{3,2,1,0:T(8,128)(2,1)S(1)}, u32[]{:S(2)}, u32[]{:S(2)}) collective-permute-start(bf16[2,4,256,128]{3,2,1,0:T(8,128)(2,1)S(1)} %get-tuple-element.15), channel_id=1, source_target_pairs={{0,8},{8,16},{16,24},{24,0},{1,9},{9,17},{17,25},{25,1},{2,10},{10... | collective-permute-start | bytes 1572872 | tf_op jit(solution)/shard_map/ppermute | solution.py:617
  28.5 6.9 %collective-permute-start.5 = (bf16[320,128]{1,0:T(8,128)(2,1)S(1)}, bf16[320,128]{1,0:T(8,128)(2,1)S(1)}, u32[]{:S(2)}, u32[]{:S(2)}) collective-permute-start(bf16[320,128]{1,0:T(8,128)(2,1)S(1)} %get-tuple-element.26), channel_id=1, source_target_pairs={{0,7},{1,0},{2,1},{3,2},{4,3},{5,4},{6,5},{7,6},{8,15},{9,8},{10,9... | collective-permute-start | bytes 245768 | tf_op jit(solution)/shard_map/ppermute | solution.py:617
  32.8 7.5 %collective-permute-start.4 = (bf16[320,128]{1,0:T(8,128)(2,1)S(1)}, bf16[320,128]{1,0:T(8,128)(2,1)S(1)}, u32[]{:S(2)}, u32[]{:S(2)}) collective-permute-start(bf16[320,128]{1,0:T(8,128)(2,1)S(1)} %get-tuple-element.27), channel_id=1, source_target_pairs={{0,1},{1,2},{2,3},{3,4},{4,5},{5,6},{6,7},{7,0},{8,9},{9,10},{10,1... | collective-permute-start | bytes 245768 | tf_op jit(solution)/shard_map/ppermute | solution.py:617

commit v3 on v2

--- a/solution.py
+++ b/solution.py
@@ -116,7 +116,13 @@
             line_ref[d, n] = line[n]
         return carry
 
-    lax.fori_loop(0, owners, product, 0, unroll=8)
+    slots, around = pl.ds(0, tail), pl.ds(tail, 32)
+    copies = []
+    for h in range(2):
+        first, last = h * owners // 2, (h + 1) * owners // 2
+        lax.fori_loop(first, last, product, 0, unroll=16)
+        part = pl.ds(first, last - first)
+        copies += fetch([out_ref.at[part, slots, :]], [out_any.at[part, slots, :]], sems.at[pl.ds(h, 1)])
     inside = lane % half
     in_rows = (inside >= 4) & (inside < 4 + 2 * rows)
     before = (inside >= 2) & (inside < 4)
@@ -136,8 +142,8 @@
         out_ref[d, pl.ds(tail, 32), :] = jnp.concatenate(parts, axis=0).astype(BF16)
         return carry
 
-    lax.fori_loop(0, owners, surround, 0, unroll=4)
-    finish(fetch([out_ref], [out_any], sems))
+    lax.fori_loop(0, owners, surround, 0, unroll=8)
+    finish(copies + fetch([out_ref.at[:, around, :]], [out_any.at[:, around, :]], sems.at[pl.ds(2, 1)]))
 
 
 def regrid(block_dest, block_row, met_src, weights, n_face, n_tile, rows):
@@ -387,21 +393,22 @@
     lax.fori_loop(0, padded // 16, group, 0, unroll=2)
 
 
-def gather_fields(came_ref, label_v, label_s, total, beside, sem):
+def read_labels(came_ref, label_v, beside):
     owners, _, cells = came_ref.shape
-    levfields = (came_ref.shape[1] - 32) // CAP
-    rows = total.shape[0] // levfields - 1
-    tail = CAP * levfields
+    tail = came_ref.shape[1] - 32
 
     def read(d, sums):
         x = came_ref[d, pl.ds(tail, 32), :].astype(F32)
         label_v[pl.ds(d, 1), :] = x[0:1].astype(jnp.int32)
         return sums + x
 
-    beside[...] = lax.fori_loop(0, owners, read, jnp.zeros((32, cells), F32), unroll=4)
-    copies = fetch([label_v], [label_s], sem)
-    total[...] = jnp.zeros_like(total)
-    finish(copies)
+    beside[...] = lax.fori_loop(0, owners, read, jnp.zeros((32, cells), F32), unroll=8)
+
+
+def add_slots(came_ref, label_s, total):
+    owners = came_ref.shape[0]
+    levfields = (came_ref.shape[1] - 32) // CAP
+    rows = total.shape[0] // levfields - 1
 
     def add(d, carry):
         for k in range(CAP):
@@ -439,12 +446,21 @@
         [came_ref, rate_ref, west_ref, east_ref, right_ref, left_ref, below_ref, above_ref], in_sems,
     )
     parts = [pl.ds(level * rows, rows) for level in range(levels)]
+    sub, lane = sublanes((cells, cells)), lanes((cells, cells))
+    finish(small[:1])
     fetch([planes_any.at[p] for p in parts], [planes.at[p] for p in parts], plane_sems)
-    sub, lane = sublanes((cells, cells)), lanes((cells, cells))
+    read_labels(came_ref, label_v, ghost)
+    label_copy = fetch([label_v], [label_s], in_sems)
+    total[...] = jnp.zeros_like(total)
     low_mask[...] = jnp.where(sub == lane - 1, 1.0, 0.0).astype(BF16)
     high_mask[...] = jnp.where(sub == lane + 1, 1.0, 0.0).astype(BF16)
-    finish(small[:1])
-    gather_fields(came_ref, label_v, label_s, total, ghost, in_sems)
+    finish(small[1:])
+    packed = padded // 8
+    place_corners(levels, [
+        ref[pl.ds(padded + n * packed, packed), :] for n in range(2) for ref in (west_ref, east_ref)
+    ], corner_ref)
+    finish(label_copy)
+    add_slots(came_ref, label_s, total)
     for fl in range(levfields):
         for r in range(0, rows, 8):
             tile_ref[fl, pl.ds(r, 8), :] = total[pl.ds(r * levfields + fl, 8, stride=levfields), :]
@@ -459,14 +475,9 @@
         x = jnp.concatenate([x, light, jnp.zeros((16 - levels, cells), F32)], axis=0)
         high = x.astype(BF16)
         rest = (x - high.astype(F32)).astype(BF16)
-        factor[r] = jnp.concatenate([high, rest, high], axis=0)
+        factor[r // 2, :, pl.ds(r % 2 * cells, cells)] = jnp.concatenate([high, rest, high], axis=0)
     line.append(ghosts[16:24])
     make_weights(levels, line, ghosts[0:8], turn(ghosts[0:8], cells // 2), inner, side, edge)
-    finish(small[1:])
-    packed = padded // 8
-    place_corners(levels, [
-        ref[pl.ds(padded + n * packed, packed), :] for n in range(2) for ref in (west_ref, east_ref)
-    ], corner_ref)
     side_columns(rows, levels, right_ref, left_ref, west_ref, east_ref, edge, mid_ref, corner_ref, next_ref)
     sub16, lane16 = sublanes((16, cells)), lanes((16, cells))
 
@@ -490,6 +501,13 @@
         x, up, down = (v.reshape(count, 8, cells) for v in (x, up, down))
         return (stay * x + up_w * up + down_w * down).reshape(count * 8, cells)
 
+    def send(level, first, last):
+        for r in range(first, last):
+            k = level * rows + r
+            pltpu.make_async_copy(
+                planes.at[k, pl.ds(0, species), :], out_any.at[:, k, 0, :], out_sems.at[k]
+            ).start()
+
     def one_level(level, carry):
         part = pl.ds(level * rows, rows)
         pltpu.make_async_copy(planes_any.at[part], planes.at[part], plane_sems.at[level]).wait()
@@ -506,6 +524,7 @@
                     return above_ref[i - rows, level, part, :].astype(F32)
                 return planes[level * rows + i, part, :]
 
+            beside_next = next_ref[part, :]
             for i in range(-1, rows + 1):
                 x = before(i)
                 beside = (mid_ref if 0 <= i < rows else corner_ref)[part, :]
@@ -517,22 +536,22 @@
                 if 0 <= i < rows:
                     once16[i] = x.astype(BF16)
             for i in range(rows):
-                both = jnp.concatenate([once16[i], next_ref[part, :]], axis=1)
+                both = jnp.concatenate([once16[i], beside_next], axis=1)
                 across = jnp.dot(both, matrix[i + 1], preferred_element_type=F32)
                 weights = [inner[level, i + 1, c] for c in range(3)]
                 moved = weighted(weights, once[i + 1], once[i + 2], once[i]) + across
-                exponent = jnp.dot(rate_ref[level, part, :], factor[i], preferred_element_type=F32)
+                if i % 2 == 0:
+                    exponents = jnp.dot(rate_ref[level, part, :], factor[i // 2], preferred_element_type=F32)
+                exponent = exponents[:, i % 2 * cells : (i % 2 + 1) * cells]
                 planes[level * rows + i, part, :] = moved * pl.reciprocal(
                     1.0 + softplus(exponent), approx=False
                 )
+                if i == rows // 2 and HALF == padded:
+                    send(level, 0, rows // 2)
             return carry
 
         lax.fori_loop(0, padded // HALF, half, 0)
-        for r in range(rows):
-            k = level * rows + r
-            pltpu.make_async_copy(
-                planes.at[k, pl.ds(0, species), :], out_any.at[:, k, 0, :], out_sems.at[k]
-            ).start()
+        send(level, rows // 2 if HALF == padded else 0, rows)
         return carry
 
     lax.fori_loop(0, levels, one_level, 0)
@@ -562,7 +581,7 @@
             pltpu.VMEM((count, padded, cells), F32),
             *buffers(small), *buffers([tile]),
             pltpu.VMEM(((rows + 1) * levfields, cells), F32),
-            pltpu.VMEM((rows, rate.shape[2], cells), BF16),
+            pltpu.VMEM((rows // 2, rate.shape[2], 2 * cells), BF16),
             pltpu.VMEM((owners, cells), jnp.int32), pltpu.SMEM((owners, cells), jnp.int32),
             pltpu.VMEM((32, cells), F32),
             pltpu.VMEM((levels, rows + 2, 3, 8, cells), F32),

time: 56.9 us -> 55.4 us (0.974)
  Pallas kernels: 30.5 us -> 29 us
    pallas_call x1, Pallas kernels: 5.33 us -> 4.12 us  [regrid(): pl.pallas_call(functools.partial(regrid_kernel, n_tile, rows), out_shape=...]
where the time goes in v3:
time: 55.4 us; the launch traced here: 55.1 us
  Pallas kernels  29 us (52%)
  starting transfers between devices  14.9 us (27%)
  waiting for transfers between devices  9.58 us (17%)
  between operations  0.79 us (1%)
  other arithmetic  0.61 us (1%)
    pallas_call x1, Pallas kernels, advect(): pl.pallas_call(functools.partial(advect_kernel, levels), out_shape=(jax.S...  13.7 us
    pallas_call x1, Pallas kernels, columns(): pl.pallas_call(functools.partial(column_kernel, levels), out_shape=(jax.S...  7.97 us
    ppermute x6, starting transfers between devices, shift(): return lax.ppermute(x, axis, [(i, (i + by) % count) for i in range(count)])  7.64 us
    all_to_all x1, starting transfers between devices, local(): lax.all_to_all(payload, ('face', 'tile'), split_axis=0, concat_axis=0, ti...  7.3 us
    ppermute x6, waiting for transfers between devices, shift(): return lax.ppermute(x, axis, [(i, (i + by) % count) for i in range(count)])  7.26 us
    pallas_call x1, Pallas kernels, regrid(): pl.pallas_call(functools.partial(regrid_kernel, n_tile, rows), out_shape=...  4.12 us
    pallas_call x1, Pallas kernels, border_rows(): pl.pallas_call(functools.partial(row_kernel, rows), out_shape=(line, line...  3.15 us
    all_to_all x1, waiting for transfers between devices, local(): lax.all_to_all(payload, ('face', 'tile'), split_axis=0, concat_axis=0, ti...  2.33 us
  transfers between devices with their start and end apart: 7, of which 3 were waited for; matrix products, arithmetic and copies ran while one was open for 2% of the time, Pallas kernels for 20%

profile of v3, /device:TPU:0, one launch (start us, length us, event | category | flops | bytes accessed | tf_op | source)
XLA Modules:
  0.0 55.1 jit_solution(9347585726402130278)
XLA Ops:
  0.6 0.0 copy-start
  0.6 0.0 copy-start.1
  0.7 4.1 %regrid.1 = bf16[32,128,128]{2,1,0:T(8,128)(2,1)} custom-call(s32[64]{0:T(128)} %dest_any.1, s32[64]{0:T(128)} %row_any.1, bf16[64,48,128]{2,1,0:T(8,128)(2,1)} %src_any.1, bf16[64,128,128]{2,1,0:T(8,128)(2,1)} %weight_any.1), custom_call_target="tpu_custom_call" | custom-call | flops 100663296 | bytes 6291456 | tf_op jit(solution)/shard_map/regrid/pallas_call | solution.py:153
  4.8 7.3 %all-to-all-start = ((bf16[32,128,128]{2,1,0:T(8,128)(2,1)}), bf16[32,128,128]{2,1,0:T(8,128)(2,1)S(1)}, u32[]{:S(2)}, u32[]{:S(2)}) async-start(bf16[32,128,128]{2,1,0:T(8,128)(2,1)} %regrid.1), calls=%async_computation | async-start | bytes 2097152 | tf_op jit(solution)/shard_map/all_to_all | solution.py:647
  12.1 3.1 %border_rows.1 = (bf16[2,4,256,128]{3,2,1,0:T(8,128)(2,1)}, bf16[2,4,256,128]{3,2,1,0:T(8,128)(2,1)S(1)}, bf16[32,128]{1,0:T(8,128)(2,1)S(1)}) custom-call(f32[250,64,1,128]{3,2,1,0:T(1,128)} %bitcast.6), custom_call_target="tpu_custom_call" | custom-call | flops 2048000 | bytes 2048000 | tf_op jit(solution)/shard_map/border_rows/pallas_call | solution.py:209
  15.2 1.6 %collective-permute-start.3 = (bf16[32,128]{1,0:T(8,128)(2,1)S(1)}, bf16[32,128]{1,0:T(8,128)(2,1)S(1)}, u32[]{:S(2)}, u32[]{:S(2)}) collective-permute-start(bf16[32,128]{1,0:T(8,128)(2,1)S(1)} %get-tuple-element.20), channel_id=1, source_target_pairs={{0,24},{8,0},{16,8},{24,16},{1,25},{9,1},{17,9},{25,17},{2,26},{10... | collective-permute-start | bytes 24584 | tf_op jit(solution)/shard_map/ppermute | solution.py:636
  16.8 0.0 collective-permute-start.2
  16.8 1.7 %collective-permute-start.1 = (bf16[2,4,256,128]{3,2,1,0:T(8,128)(2,1)}, bf16[2,4,256,128]{3,2,1,0:T(8,128)(2,1)S(1)}, u32[]{:S(2)}, u32[]{:S(2)}) collective-permute-start(bf16[2,4,256,128]{3,2,1,0:T(8,128)(2,1)} %get-tuple-element.14), channel_id=1, source_target_pairs={{0,24},{8,0},{16,8},{24,16},{1,25},{9,1},{17,9},{25,17},{2,26},{10... | collective-permute-start | bytes 1572872 | tf_op jit(solution)/shard_map/ppermute | solution.py:636
  18.6 0.0 collective-permute-start
  18.6 0.0 copy-done
  18.6 0.1 broadcast_multiply_fusion
  18.8 0.0 copy-done.1
  18.8 0.1 broadcast_multiply_fusion.1
  18.8 0.1 pad_maximum_fusion.1
  18.9 0.2 copy.13
  19.1 0.1 reduce-precision_convert_fusion
  19.2 8.0 %columns.1 = (f32[64,256,128]{2,1,0:T(8,128)}, bf16[256,128]{1,0:T(8,128)(2,1)S(1)}, bf16[256,128]{1,0:T(8,128)(2,1)S(1)}) custom-call(f32[250,64,1,128]{3,2,1,0:T(1,128)} %bitcast.7), custom_call_target="tpu_custom_call" | custom-call | flops 24576000 | bytes 8192000 | tf_op jit(solution)/shard_map/columns/pallas_call | solution.py:275
  27.2 0.0 collective-permute-done.3
  27.2 0.0 collective-permute-done.2
  27.3 4.3 %collective-permute-start.5 = (bf16[320,128]{1,0:T(8,128)(2,1)S(1)}, bf16[320,128]{1,0:T(8,128)(2,1)S(1)}, u32[]{:S(2)}, u32[]{:S(2)}) collective-permute-start(bf16[320,128]{1,0:T(8,128)(2,1)S(1)} %get-tuple-element.26), channel_id=1, source_target_pairs={{0,7},{1,0},{2,1},{3,2},{4,3},{5,4},{6,5},{7,6},{8,15},{9,8},{10,9... | collective-permute-start | bytes 245768 | tf_op jit(solution)/shard_map/ppermute | solution.py:636
  31.6 0.0 collective-permute-start.4
  31.6 0.3 pad_maximum_fusion.rate_any
  31.8 2.3 %collective-permute-done.5.refs_1_.east_any = bf16[320,128]{1,0:T(8,128)(2,1)S(1)} collective-permute-done((bf16[320,128]{1,0:T(8,128)(2,1)S(1)}, bf16[320,128]{1,0:T(8,128)(2,1)S(1)}, u32[]{:S(2)}, u32[]{:S(2)}) %collective-permute-start.5) | collective-permute-done | bytes 81952 | tf_op jit(solution)/shard_map/ppermute | solution.py:636
  34.1 5.0 %collective-permute-done.4.refs_0_.west_any = bf16[320,128]{1,0:T(8,128)(2,1)S(1)} collective-permute-done((bf16[320,128]{1,0:T(8,128)(2,1)S(1)}, bf16[320,128]{1,0:T(8,128)(2,1)S(1)}, u32[]{:S(2)}, u32[]{:S(2)}) %collective-permute-start.4) | collective-permute-done | bytes 81952 | tf_op jit(solution)/shard_map/ppermute | solution.py:636
  39.1 0.0 collective-permute-done.1.refs_1_.above_any
  39.1 0.0 collective-permute-done.refs_0_.below_any
  39.1 2.3 %all-to-all-done.came_any = bf16[32,128,128]{2,1,0:T(8,128)(2,1)S(1)} async-done(((bf16[32,128,128]{2,1,0:T(8,128)(2,1)}), bf16[32,128,128]{2,1,0:T(8,128)(2,1)S(1)}, u32[]{:S(2)}, u32[]{:S(2)}) %all-to-all-start) | async-done | bytes 1048608 | tf_op jit(solution)/shard_map/all_to_all | solution.py:647
  41.4 13.7 %advect.1 = (f32[250,64,1,128]{3,2,1,0:T(1,128)}, f32[48,16,128]{2,1,0:T(8,128)}) custom-call(f32[64,256,128]{2,1,0:T(8,128)} %get-tuple-element.17.planes_any, bf16[2,4,256,128]{3,2,1,0:T(8,128)(2,1)S(1)} %collective-permute-done.refs_0_.below_any, bf16[2,4,256,128]{3,2,1,0:T(8,128)(2,1)S(1)} %collective-permute-done.1.refs_1_.above_any, ...), custom_call_target="tpu_custom_call" | custom-call | flops 125829120 | bytes 16777216 | tf_op jit(solution)/shard_map/advect/pallas_call | solution.py:575
  (7 shorter events, 0.1 us)
Async XLA Ops:
  0.6 17.9 %copy-start = (f32[250,12]{0,1:T(8,128)S(1)}, f32[250,12]{0,1:T(8,128)}, u32[]{:S(2)}) copy-start(f32[250,12]{0,1:T(8,128)} %param.12) | copy-start | bytes 36004
  0.6 18.1 %copy-start.1 = (f32[250]{0:T(256)S(1)}, f32[250]{0:T(256)}, u32[]{:S(2)}) copy-start(f32[250]{0:T(256)} %param.13) | copy-start | bytes 3004
  4.8 36.7 %all-to-all-start = ((bf16[32,128,128]{2,1,0:T(8,128)(2,1)}), bf16[32,128,128]{2,1,0:T(8,128)(2,1)S(1)}, u32[]{:S(2)}, u32[]{:S(2)}) async-start(bf16[32,128,128]{2,1,0:T(8,128)(2,1)} %regrid.1), calls=%async_computation | async-start | bytes 2097152 | tf_op jit(solution)/shard_map/all_to_all | solution.py:647
  15.2 12.0 %collective-permute-start.3 = (bf16[32,128]{1,0:T(8,128)(2,1)S(1)}, bf16[32,128]{1,0:T(8,128)(2,1)S(1)}, u32[]{:S(2)}, u32[]{:S(2)}) collective-permute-start(bf16[32,128]{1,0:T(8,128)(2,1)S(1)} %get-tuple-element.20), channel_id=1, source_target_pairs={{0,24},{8,0},{16,8},{24,16},{1,25},{9,1},{17,9},{25,17},{2,26},{10... | collective-permute-start | bytes 24584 | tf_op jit(solution)/shard_map/ppermute | solution.py:636
  16.8 10.4 %collective-permute-start.2 = (bf16[32,128]{1,0:T(8,128)(2,1)S(1)}, bf16[32,128]{1,0:T(8,128)(2,1)S(1)}, u32[]{:S(2)}, u32[]{:S(2)}) collective-permute-start(bf16[32,128]{1,0:T(8,128)(2,1)S(1)} %get-tuple-element.20), channel_id=1, source_target_pairs={{0,8},{8,16},{16,24},{24,0},{1,9},{9,17},{17,25},{25,1},{2,10},{10... | collective-permute-start | bytes 24584 | tf_op jit(solution)/shard_map/ppermute | solution.py:636
  16.8 22.3 %collective-permute-start.1 = (bf16[2,4,256,128]{3,2,1,0:T(8,128)(2,1)}, bf16[2,4,256,128]{3,2,1,0:T(8,128)(2,1)S(1)}, u32[]{:S(2)}, u32[]{:S(2)}) collective-permute-start(bf16[2,4,256,128]{3,2,1,0:T(8,128)(2,1)} %get-tuple-element.14), channel_id=1, source_target_pairs={{0,24},{8,0},{16,8},{24,16},{1,25},{9,1},{17,9},{25,17},{2,26},{10... | collective-permute-start | bytes 1572872 | tf_op jit(solution)/shard_map/ppermute | solution.py:636
  18.6 20.5 %collective-permute-start = (bf16[2,4,256,128]{3,2,1,0:T(8,128)(2,1)S(1)}, bf16[2,4,256,128]{3,2,1,0:T(8,128)(2,1)S(1)}, u32[]{:S(2)}, u32[]{:S(2)}) collective-permute-start(bf16[2,4,256,128]{3,2,1,0:T(8,128)(2,1)S(1)} %get-tuple-element.15), channel_id=1, source_target_pairs={{0,8},{8,16},{16,24},{24,0},{1,9},{9,17},{17,25},{25,1},{2,10},{10... | collective-permute-start | bytes 1572872 | tf_op jit(solution)/shard_map/ppermute | solution.py:636
  27.3 6.9 %collective-permute-start.5 = (bf16[320,128]{1,0:T(8,128)(2,1)S(1)}, bf16[320,128]{1,0:T(8,128)(2,1)S(1)}, u32[]{:S(2)}, u32[]{:S(2)}) collective-permute-start(bf16[320,128]{1,0:T(8,128)(2,1)S(1)} %get-tuple-element.26), channel_id=1, source_target_pairs={{0,7},{1,0},{2,1},{3,2},{4,3},{5,4},{6,5},{7,6},{8,15},{9,8},{10,9... | collective-permute-start | bytes 245768 | tf_op jit(solution)/shard_map/ppermute | solution.py:636
  31.6 7.5 %collective-permute-start.4 = (bf16[320,128]{1,0:T(8,128)(2,1)S(1)}, bf16[320,128]{1,0:T(8,128)(2,1)S(1)}, u32[]{:S(2)}, u32[]{:S(2)}) collective-permute-start(bf16[320,128]{1,0:T(8,128)(2,1)S(1)} %get-tuple-element.27), channel_id=1, source_target_pairs={{0,1},{1,2},{2,3},{3,4},{4,5},{5,6},{6,7},{7,0},{8,9},{9,10},{10,1... | collective-permute-start | bytes 245768 | tf_op jit(solution)/shard_map/ppermute | solution.py:636

commit v4 on v3

--- a/solution.py
+++ b/solution.py
@@ -390,7 +390,7 @@
         next_ref[part, :] = after.astype(BF16)
         return carry
 
-    lax.fori_loop(0, padded // 16, group, 0, unroll=2)
+    lax.fori_loop(0, padded // 16, group, 0, unroll=8)
 
 
 def read_labels(came_ref, label_v, beside):
@@ -402,7 +402,7 @@
         label_v[pl.ds(d, 1), :] = x[0:1].astype(jnp.int32)
         return sums + x
 
-    beside[...] = lax.fori_loop(0, owners, read, jnp.zeros((32, cells), F32), unroll=8)
+    beside[...] = lax.fori_loop(0, owners, read, jnp.zeros((32, cells), F32), unroll=16)
 
 
 def add_slots(came_ref, label_s, total):
@@ -416,7 +416,7 @@
             total[pl.ds(at, levfields), :] += came_ref[d, pl.ds(k * levfields, levfields), :].astype(F32)
         return carry
 
-    lax.fori_loop(0, owners, add, 0, unroll=4)
+    lax.fori_loop(0, owners, add, 0, unroll=16)
 
 
 def light_of(levels, optical):

time: 55.4 us -> 55.1 us (level)
  no operation moved by 1% of the time
where the time goes in v4:
time: 55.1 us; the launch traced here: 54.8 us
  Pallas kernels  28.6 us (52%)
  starting transfers between devices  14.9 us (27%)
  waiting for transfers between devices  9.58 us (17%)
  between operations  0.79 us (1%)
  other arithmetic  0.61 us (1%)
    pallas_call x1, Pallas kernels, advect(): pl.pallas_call(functools.partial(advect_kernel, levels), out_shape=(jax.S...  13.3 us
    pallas_call x1, Pallas kernels, columns(): pl.pallas_call(functools.partial(column_kernel, levels), out_shape=(jax.S...  7.97 us
    ppermute x6, starting transfers between devices, shift(): return lax.ppermute(x, axis, [(i, (i + by) % count) for i in range(count)])  7.64 us
    all_to_all x1, starting transfers between devices, local(): lax.all_to_all(payload, ('face', 'tile'), split_axis=0, concat_axis=0, ti...  7.3 us
    ppermute x6, waiting for transfers between devices, shift(): return lax.ppermute(x, axis, [(i, (i + by) % count) for i in range(count)])  7.26 us
    pallas_call x1, Pallas kernels, regrid(): pl.pallas_call(functools.partial(regrid_kernel, n_tile, rows), out_shape=...  4.12 us
    pallas_call x1, Pallas kernels, border_rows(): pl.pallas_call(functools.partial(row_kernel, rows), out_shape=(line, line...  3.15 us
    all_to_all x1, waiting for transfers between devices, local(): lax.all_to_all(payload, ('face', 'tile'), split_axis=0, concat_axis=0, ti...  2.32 us
  transfers between devices with their start and end apart: 7, of which 3 were waited for; matrix products, arithmetic and copies ran while one was open for 2% of the time, Pallas kernels for 20%

profile of v4, /device:TPU:0, one launch (start us, length us, event | category | flops | bytes accessed | tf_op | source)
XLA Modules:
  0.0 54.8 jit_solution(11033926742597379542)
XLA Ops:
  0.6 0.0 copy-start
  0.6 0.0 copy-start.1
  0.7 4.1 %regrid.1 = bf16[32,128,128]{2,1,0:T(8,128)(2,1)} custom-call(s32[64]{0:T(128)} %dest_any.1, s32[64]{0:T(128)} %row_any.1, bf16[64,48,128]{2,1,0:T(8,128)(2,1)} %src_any.1, bf16[64,128,128]{2,1,0:T(8,128)(2,1)} %weight_any.1), custom_call_target="tpu_custom_call" | custom-call | flops 100663296 | bytes 6291456 | tf_op jit(solution)/shard_map/regrid/pallas_call | solution.py:153
  4.8 7.3 %all-to-all-start = ((bf16[32,128,128]{2,1,0:T(8,128)(2,1)}), bf16[32,128,128]{2,1,0:T(8,128)(2,1)S(1)}, u32[]{:S(2)}, u32[]{:S(2)}) async-start(bf16[32,128,128]{2,1,0:T(8,128)(2,1)} %regrid.1), calls=%async_computation | async-start | bytes 2097152 | tf_op jit(solution)/shard_map/all_to_all | solution.py:647
  12.1 3.1 %border_rows.1 = (bf16[2,4,256,128]{3,2,1,0:T(8,128)(2,1)}, bf16[2,4,256,128]{3,2,1,0:T(8,128)(2,1)S(1)}, bf16[32,128]{1,0:T(8,128)(2,1)S(1)}) custom-call(f32[250,64,1,128]{3,2,1,0:T(1,128)} %bitcast.6), custom_call_target="tpu_custom_call" | custom-call | flops 2048000 | bytes 2048000 | tf_op jit(solution)/shard_map/border_rows/pallas_call | solution.py:209
  15.2 1.6 %collective-permute-start.3 = (bf16[32,128]{1,0:T(8,128)(2,1)S(1)}, bf16[32,128]{1,0:T(8,128)(2,1)S(1)}, u32[]{:S(2)}, u32[]{:S(2)}) collective-permute-start(bf16[32,128]{1,0:T(8,128)(2,1)S(1)} %get-tuple-element.20), channel_id=1, source_target_pairs={{0,24},{8,0},{16,8},{24,16},{1,25},{9,1},{17,9},{25,17},{2,26},{10... | collective-permute-start | bytes 24584 | tf_op jit(solution)/shard_map/ppermute | solution.py:636
  16.8 0.0 collective-permute-start.2
  16.8 1.7 %collective-permute-start.1 = (bf16[2,4,256,128]{3,2,1,0:T(8,128)(2,1)}, bf16[2,4,256,128]{3,2,1,0:T(8,128)(2,1)S(1)}, u32[]{:S(2)}, u32[]{:S(2)}) collective-permute-start(bf16[2,4,256,128]{3,2,1,0:T(8,128)(2,1)} %get-tuple-element.14), channel_id=1, source_target_pairs={{0,24},{8,0},{16,8},{24,16},{1,25},{9,1},{17,9},{25,17},{2,26},{10... | collective-permute-start | bytes 1572872 | tf_op jit(solution)/shard_map/ppermute | solution.py:636
  18.6 0.0 collective-permute-start
  18.6 0.0 copy-done
  18.6 0.1 broadcast_multiply_fusion
  18.8 0.0 copy-done.1
  18.8 0.1 broadcast_multiply_fusion.1
  18.8 0.1 pad_maximum_fusion.1
  18.9 0.2 copy.13
  19.1 0.1 reduce-precision_convert_fusion
  19.2 8.0 %columns.1 = (f32[64,256,128]{2,1,0:T(8,128)}, bf16[256,128]{1,0:T(8,128)(2,1)S(1)}, bf16[256,128]{1,0:T(8,128)(2,1)S(1)}) custom-call(f32[250,64,1,128]{3,2,1,0:T(1,128)} %bitcast.7), custom_call_target="tpu_custom_call" | custom-call | flops 24576000 | bytes 8192000 | tf_op jit(solution)/shard_map/columns/pallas_call | solution.py:275
  27.2 0.0 collective-permute-done.3
  27.2 0.0 collective-permute-done.2
  27.3 4.3 %collective-permute-start.5 = (bf16[320,128]{1,0:T(8,128)(2,1)S(1)}, bf16[320,128]{1,0:T(8,128)(2,1)S(1)}, u32[]{:S(2)}, u32[]{:S(2)}) collective-permute-start(bf16[320,128]{1,0:T(8,128)(2,1)S(1)} %get-tuple-element.26), channel_id=1, source_target_pairs={{0,7},{1,0},{2,1},{3,2},{4,3},{5,4},{6,5},{7,6},{8,15},{9,8},{10,9... | collective-permute-start | bytes 245768 | tf_op jit(solution)/shard_map/ppermute | solution.py:636
  31.6 0.0 collective-permute-start.4
  31.6 0.3 pad_maximum_fusion.rate_any
  31.8 2.3 %collective-permute-done.5.refs_1_.east_any = bf16[320,128]{1,0:T(8,128)(2,1)S(1)} collective-permute-done((bf16[320,128]{1,0:T(8,128)(2,1)S(1)}, bf16[320,128]{1,0:T(8,128)(2,1)S(1)}, u32[]{:S(2)}, u32[]{:S(2)}) %collective-permute-start.5) | collective-permute-done | bytes 81952 | tf_op jit(solution)/shard_map/ppermute | solution.py:636
  34.1 5.0 %collective-permute-done.4.refs_0_.west_any = bf16[320,128]{1,0:T(8,128)(2,1)S(1)} collective-permute-done((bf16[320,128]{1,0:T(8,128)(2,1)S(1)}, bf16[320,128]{1,0:T(8,128)(2,1)S(1)}, u32[]{:S(2)}, u32[]{:S(2)}) %collective-permute-start.4) | collective-permute-done | bytes 81952 | tf_op jit(solution)/shard_map/ppermute | solution.py:636
  39.1 0.0 collective-permute-done.1.refs_1_.above_any
  39.1 0.0 collective-permute-done.refs_0_.below_any
  39.1 2.3 %all-to-all-done.came_any = bf16[32,128,128]{2,1,0:T(8,128)(2,1)S(1)} async-done(((bf16[32,128,128]{2,1,0:T(8,128)(2,1)}), bf16[32,128,128]{2,1,0:T(8,128)(2,1)S(1)}, u32[]{:S(2)}, u32[]{:S(2)}) %all-to-all-start) | async-done | bytes 1048608 | tf_op jit(solution)/shard_map/all_to_all | solution.py:647
  41.4 13.3 %advect.1 = (f32[250,64,1,128]{3,2,1,0:T(1,128)}, f32[48,16,128]{2,1,0:T(8,128)}) custom-call(f32[64,256,128]{2,1,0:T(8,128)} %get-tuple-element.17.planes_any, bf16[2,4,256,128]{3,2,1,0:T(8,128)(2,1)S(1)} %collective-permute-done.refs_0_.below_any, bf16[2,4,256,128]{3,2,1,0:T(8,128)(2,1)S(1)} %collective-permute-done.1.refs_1_.above_any, ...), custom_call_target="tpu_custom_call" | custom-call | flops 125829120 | bytes 16777216 | tf_op jit(solution)/shard_map/advect/pallas_call | solution.py:575
  (7 shorter events, 0.1 us)
Async XLA Ops:
  0.6 17.9 %copy-start = (f32[250,12]{0,1:T(8,128)S(1)}, f32[250,12]{0,1:T(8,128)}, u32[]{:S(2)}) copy-start(f32[250,12]{0,1:T(8,128)} %param.12) | copy-start | bytes 36004
  0.6 18.1 %copy-start.1 = (f32[250]{0:T(256)S(1)}, f32[250]{0:T(256)}, u32[]{:S(2)}) copy-start(f32[250]{0:T(256)} %param.13) | copy-start | bytes 3004
  4.8 36.7 %all-to-all-start = ((bf16[32,128,128]{2,1,0:T(8,128)(2,1)}), bf16[32,128,128]{2,1,0:T(8,128)(2,1)S(1)}, u32[]{:S(2)}, u32[]{:S(2)}) async-start(bf16[32,128,128]{2,1,0:T(8,128)(2,1)} %regrid.1), calls=%async_computation | async-start | bytes 2097152 | tf_op jit(solution)/shard_map/all_to_all | solution.py:647
  15.2 12.0 %collective-permute-start.3 = (bf16[32,128]{1,0:T(8,128)(2,1)S(1)}, bf16[32,128]{1,0:T(8,128)(2,1)S(1)}, u32[]{:S(2)}, u32[]{:S(2)}) collective-permute-start(bf16[32,128]{1,0:T(8,128)(2,1)S(1)} %get-tuple-element.20), channel_id=1, source_target_pairs={{0,24},{8,0},{16,8},{24,16},{1,25},{9,1},{17,9},{25,17},{2,26},{10... | collective-permute-start | bytes 24584 | tf_op jit(solution)/shard_map/ppermute | solution.py:636
  16.8 10.4 %collective-permute-start.2 = (bf16[32,128]{1,0:T(8,128)(2,1)S(1)}, bf16[32,128]{1,0:T(8,128)(2,1)S(1)}, u32[]{:S(2)}, u32[]{:S(2)}) collective-permute-start(bf16[32,128]{1,0:T(8,128)(2,1)S(1)} %get-tuple-element.20), channel_id=1, source_target_pairs={{0,8},{8,16},{16,24},{24,0},{1,9},{9,17},{17,25},{25,1},{2,10},{10... | collective-permute-start | bytes 24584 | tf_op jit(solution)/shard_map/ppermute | solution.py:636
  16.8 22.3 %collective-permute-start.1 = (bf16[2,4,256,128]{3,2,1,0:T(8,128)(2,1)}, bf16[2,4,256,128]{3,2,1,0:T(8,128)(2,1)S(1)}, u32[]{:S(2)}, u32[]{:S(2)}) collective-permute-start(bf16[2,4,256,128]{3,2,1,0:T(8,128)(2,1)} %get-tuple-element.14), channel_id=1, source_target_pairs={{0,24},{8,0},{16,8},{24,16},{1,25},{9,1},{17,9},{25,17},{2,26},{10... | collective-permute-start | bytes 1572872 | tf_op jit(solution)/shard_map/ppermute | solution.py:636
  18.6 20.5 %collective-permute-start = (bf16[2,4,256,128]{3,2,1,0:T(8,128)(2,1)S(1)}, bf16[2,4,256,128]{3,2,1,0:T(8,128)(2,1)S(1)}, u32[]{:S(2)}, u32[]{:S(2)}) collective-permute-start(bf16[2,4,256,128]{3,2,1,0:T(8,128)(2,1)S(1)} %get-tuple-element.15), channel_id=1, source_target_pairs={{0,8},{8,16},{16,24},{24,0},{1,9},{9,17},{17,25},{25,1},{2,10},{10... | collective-permute-start | bytes 1572872 | tf_op jit(solution)/shard_map/ppermute | solution.py:636
  27.3 6.9 %collective-permute-start.5 = (bf16[320,128]{1,0:T(8,128)(2,1)S(1)}, bf16[320,128]{1,0:T(8,128)(2,1)S(1)}, u32[]{:S(2)}, u32[]{:S(2)}) collective-permute-start(bf16[320,128]{1,0:T(8,128)(2,1)S(1)} %get-tuple-element.26), channel_id=1, source_target_pairs={{0,7},{1,0},{2,1},{3,2},{4,3},{5,4},{6,5},{7,6},{8,15},{9,8},{10,9... | collective-permute-start | bytes 245768 | tf_op jit(solution)/shard_map/ppermute | solution.py:636
  31.6 7.5 %collective-permute-start.4 = (bf16[320,128]{1,0:T(8,128)(2,1)S(1)}, bf16[320,128]{1,0:T(8,128)(2,1)S(1)}, u32[]{:S(2)}, u32[]{:S(2)}) collective-permute-start(bf16[320,128]{1,0:T(8,128)(2,1)S(1)} %get-tuple-element.27), channel_id=1, source_target_pairs={{0,1},{1,2},{2,3},{3,4},{4,5},{5,6},{6,7},{7,0},{8,9},{9,10},{10,1... | collective-permute-start | bytes 245768 | tf_op jit(solution)/shard_map/ppermute | solution.py:636

commit v5 on v4

--- a/solution.py
+++ b/solution.py
@@ -430,9 +430,9 @@
 
 def advect_kernel(
     levels, planes_any, below_any, above_any, right_any, left_any, west_any, east_any,
-    came_any, rate_any, around_any, out_any, tile_any,
+    came_ref, rate_any, around_any, out_any, tile_any,
     planes, below_ref, above_ref, right_ref, left_ref, west_ref, east_ref,
-    came_ref, rate_ref,
+    rate_ref,
     tile_ref, total, factor, label_v, label_s, ghost,
     inner, side, edge, mid_ref, corner_ref, next_ref, matrix, low_mask, high_mask, once, once16,
     plane_sems, in_sems, out_sems,
@@ -442,19 +442,18 @@
     species = out_any.shape[0]
     span = cells // levels
     small = fetch(
-        [came_any, rate_any, west_any, east_any, right_any, left_any, below_any, above_any],
-        [came_ref, rate_ref, west_ref, east_ref, right_ref, left_ref, below_ref, above_ref], in_sems,
+        [rate_any, west_any, east_any, right_any, left_any, below_any, above_any],
+        [rate_ref, west_ref, east_ref, right_ref, left_ref, below_ref, above_ref], in_sems,
     )
     parts = [pl.ds(level * rows, rows) for level in range(levels)]
     sub, lane = sublanes((cells, cells)), lanes((cells, cells))
-    finish(small[:1])
     fetch([planes_any.at[p] for p in parts], [planes.at[p] for p in parts], plane_sems)
     read_labels(came_ref, label_v, ghost)
-    label_copy = fetch([label_v], [label_s], in_sems)
+    label_copy = fetch([label_v], [label_s], in_sems.at[pl.ds(len(small), 1)])
     total[...] = jnp.zeros_like(total)
     low_mask[...] = jnp.where(sub == lane - 1, 1.0, 0.0).astype(BF16)
     high_mask[...] = jnp.where(sub == lane + 1, 1.0, 0.0).astype(BF16)
-    finish(small[1:])
+    finish(small)
     packed = padded // 8
     place_corners(levels, [
         ref[pl.ds(padded + n * packed, packed), :] for n in range(2) for ref in (west_ref, east_ref)
@@ -569,13 +568,13 @@
     owners = came.shape[0]
     levfields = (came.shape[1] - 32) // CAP
     tile = jax.ShapeDtypeStruct((levfields, rows, cells), F32)
-    small = [below, above, right, left, west, east, came, rate]
+    small = [below, above, right, left, west, east, rate]
     column = pltpu.VMEM((padded, cells), BF16)
     square = pltpu.VMEM((cells, cells), BF16)
     return pl.pallas_call(
         functools.partial(advect_kernel, levels),
         out_shape=(jax.ShapeDtypeStruct((species, count, 1, cells), F32), tile),
-        in_specs=here(2 + len(small)),
+        in_specs=here(len(small)) + [pl.BlockSpec(memory_space=VMEM)] + here(2),
         out_specs=tuple(here(2)),
         scratch_shapes=[
             pltpu.VMEM((count, padded, cells), F32),
@@ -592,7 +591,7 @@
             square, square,
             pltpu.VMEM((rows + 2, HALF, cells), F32),
             pltpu.VMEM((rows, HALF, cells), BF16),
-            pltpu.SemaphoreType.DMA((levels,)), pltpu.SemaphoreType.DMA((len(small),)),
+            pltpu.SemaphoreType.DMA((levels,)), pltpu.SemaphoreType.DMA((len(small) + 1,)),
             pltpu.SemaphoreType.DMA((count,)),
         ],
         compiler_params=params(ADV),
@@ -600,7 +599,7 @@
             flops=60 * planes.size, bytes_accessed=8 * planes.size, transcendentals=3 * planes.size
         ),
         name="advect",
-    )(planes, *small, around)
+    )(planes, *small[:-1], came, rate, around)
 
 
 def arrived_kernel(*refs):

time: 55.1 us -> 55 us (level)
  no operation moved by 1% of the time
where the time goes in v5:
time: 55 us; the launch traced here: 54.7 us
  Pallas kernels  28.5 us (52%)
  starting transfers between devices  15 us (27%)
  waiting for transfers between devices  9.59 us (17%)
  between operations  0.79 us (1%)
  other arithmetic  0.61 us (1%)
    pallas_call x1, Pallas kernels, advect(): pl.pallas_call(functools.partial(advect_kernel, levels), out_shape=(jax.S...  13.3 us
    pallas_call x1, Pallas kernels, columns(): pl.pallas_call(functools.partial(column_kernel, levels), out_shape=(jax.S...  7.97 us
    ppermute x6, starting transfers between devices, shift(): return lax.ppermute(x, axis, [(i, (i + by) % count) for i in range(count)])  7.64 us
    all_to_all x1, starting transfers between devices, local(): lax.all_to_all(payload, ('face', 'tile'), split_axis=0, concat_axis=0, ti...  7.31 us
    ppermute x6, waiting for transfers between devices, shift(): return lax.ppermute(x, axis, [(i, (i + by) % count) for i in range(count)])  7.27 us
    pallas_call x1, Pallas kernels, regrid(): pl.pallas_call(functools.partial(regrid_kernel, n_tile, rows), out_shape=...  4.11 us
    pallas_call x1, Pallas kernels, border_rows(): pl.pallas_call(functools.partial(row_kernel, rows), out_shape=(line, line...  3.14 us
    all_to_all x1, waiting for transfers between devices, local(): lax.all_to_all(payload, ('face', 'tile'), split_axis=0, concat_axis=0, ti...  2.32 us
  transfers between devices with their start and end apart: 7, of which 3 were waited for; matrix products, arithmetic and copies ran while one was open for 2% of the time, Pallas kernels for 20%

profile of v5, /device:TPU:0, one launch (start us, length us, event | category | flops | bytes accessed | tf_op | source)
XLA Modules:
  0.0 54.7 jit_solution(12160046295172122696)
XLA Ops:
  0.6 0.0 copy-start
  0.6 0.0 copy-start.1
  0.7 4.1 %regrid.1 = bf16[32,128,128]{2,1,0:T(8,128)(2,1)} custom-call(s32[64]{0:T(128)} %dest_any.1, s32[64]{0:T(128)} %row_any.1, bf16[64,48,128]{2,1,0:T(8,128)(2,1)} %src_any.1, bf16[64,128,128]{2,1,0:T(8,128)(2,1)} %weight_any.1), custom_call_target="tpu_custom_call" | custom-call | flops 100663296 | bytes 6291456 | tf_op jit(solution)/shard_map/regrid/pallas_call | solution.py:153
  4.8 7.3 %all-to-all-start = ((bf16[32,128,128]{2,1,0:T(8,128)(2,1)}), bf16[32,128,128]{2,1,0:T(8,128)(2,1)S(1)}, u32[]{:S(2)}, u32[]{:S(2)}) async-start(bf16[32,128,128]{2,1,0:T(8,128)(2,1)} %regrid.1), calls=%async_computation | async-start | bytes 2097152 | tf_op jit(solution)/shard_map/all_to_all | solution.py:646
  12.1 3.1 %border_rows.1 = (bf16[2,4,256,128]{3,2,1,0:T(8,128)(2,1)}, bf16[2,4,256,128]{3,2,1,0:T(8,128)(2,1)S(1)}, bf16[32,128]{1,0:T(8,128)(2,1)S(1)}) custom-call(f32[250,64,1,128]{3,2,1,0:T(1,128)} %bitcast.6), custom_call_target="tpu_custom_call" | custom-call | flops 2048000 | bytes 2048000 | tf_op jit(solution)/shard_map/border_rows/pallas_call | solution.py:209
  15.2 1.6 %collective-permute-start.3 = (bf16[32,128]{1,0:T(8,128)(2,1)S(1)}, bf16[32,128]{1,0:T(8,128)(2,1)S(1)}, u32[]{:S(2)}, u32[]{:S(2)}) collective-permute-start(bf16[32,128]{1,0:T(8,128)(2,1)S(1)} %get-tuple-element.20), channel_id=1, source_target_pairs={{0,24},{8,0},{16,8},{24,16},{1,25},{9,1},{17,9},{25,17},{2,26},{10... | collective-permute-start | bytes 24584 | tf_op jit(solution)/shard_map/ppermute | solution.py:635
  16.8 0.0 collective-permute-start.2
  16.8 1.7 %collective-permute-start.1 = (bf16[2,4,256,128]{3,2,1,0:T(8,128)(2,1)}, bf16[2,4,256,128]{3,2,1,0:T(8,128)(2,1)S(1)}, u32[]{:S(2)}, u32[]{:S(2)}) collective-permute-start(bf16[2,4,256,128]{3,2,1,0:T(8,128)(2,1)} %get-tuple-element.14), channel_id=1, source_target_pairs={{0,24},{8,0},{16,8},{24,16},{1,25},{9,1},{17,9},{25,17},{2,26},{10... | collective-permute-start | bytes 1572872 | tf_op jit(solution)/shard_map/ppermute | solution.py:635
  18.6 0.0 collective-permute-start
  18.6 0.0 copy-done
  18.6 0.1 broadcast_multiply_fusion
  18.8 0.0 copy-done.1
  18.8 0.1 broadcast_multiply_fusion.1
  18.8 0.1 pad_maximum_fusion.1
  18.9 0.2 copy.13
  19.1 0.1 reduce-precision_convert_fusion
  19.2 8.0 %columns.1 = (f32[64,256,128]{2,1,0:T(8,128)}, bf16[256,128]{1,0:T(8,128)(2,1)S(1)}, bf16[256,128]{1,0:T(8,128)(2,1)S(1)}) custom-call(f32[250,64,1,128]{3,2,1,0:T(1,128)} %bitcast.7), custom_call_target="tpu_custom_call" | custom-call | flops 24576000 | bytes 8192000 | tf_op jit(solution)/shard_map/columns/pallas_call | solution.py:275
  27.2 0.0 collective-permute-done.3
  27.2 0.0 collective-permute-done.2
  27.3 4.3 %collective-permute-start.5 = (bf16[320,128]{1,0:T(8,128)(2,1)S(1)}, bf16[320,128]{1,0:T(8,128)(2,1)S(1)}, u32[]{:S(2)}, u32[]{:S(2)}) collective-permute-start(bf16[320,128]{1,0:T(8,128)(2,1)S(1)} %get-tuple-element.26), channel_id=1, source_target_pairs={{0,7},{1,0},{2,1},{3,2},{4,3},{5,4},{6,5},{7,6},{8,15},{9,8},{10,9... | collective-permute-start | bytes 245768 | tf_op jit(solution)/shard_map/ppermute | solution.py:635
  31.6 0.0 collective-permute-start.4
  31.6 0.3 pad_maximum_fusion.rate_any
  31.8 2.3 %collective-permute-done.5.refs_1_.east_any = bf16[320,128]{1,0:T(8,128)(2,1)S(1)} collective-permute-done((bf16[320,128]{1,0:T(8,128)(2,1)S(1)}, bf16[320,128]{1,0:T(8,128)(2,1)S(1)}, u32[]{:S(2)}, u32[]{:S(2)}) %collective-permute-start.5) | collective-permute-done | bytes 81952 | tf_op jit(solution)/shard_map/ppermute | solution.py:635
  34.1 5.0 %collective-permute-done.4.refs_0_.west_any = bf16[320,128]{1,0:T(8,128)(2,1)S(1)} collective-permute-done((bf16[320,128]{1,0:T(8,128)(2,1)S(1)}, bf16[320,128]{1,0:T(8,128)(2,1)S(1)}, u32[]{:S(2)}, u32[]{:S(2)}) %collective-permute-start.4) | collective-permute-done | bytes 81952 | tf_op jit(solution)/shard_map/ppermute | solution.py:635
  39.1 0.0 collective-permute-done.1.refs_1_.above_any
  39.1 0.0 collective-permute-done.refs_0_.below_any
  39.1 2.3 %all-to-all-done.came_ref = bf16[32,128,128]{2,1,0:T(8,128)(2,1)S(1)} async-done(((bf16[32,128,128]{2,1,0:T(8,128)(2,1)}), bf16[32,128,128]{2,1,0:T(8,128)(2,1)S(1)}, u32[]{:S(2)}, u32[]{:S(2)}) %all-to-all-start) | async-done | bytes 1048608 | tf_op jit(solution)/shard_map/all_to_all | solution.py:646
  41.4 13.3 %advect.1 = (f32[250,64,1,128]{3,2,1,0:T(1,128)}, f32[48,16,128]{2,1,0:T(8,128)}) custom-call(f32[64,256,128]{2,1,0:T(8,128)} %get-tuple-element.17.planes_any, bf16[2,4,256,128]{3,2,1,0:T(8,128)(2,1)S(1)} %collective-permute-done.refs_0_.below_any, bf16[2,4,256,128]{3,2,1,0:T(8,128)(2,1)S(1)} %collective-permute-done.1.refs_1_.above_any, ...), custom_call_target="tpu_custom_call" | custom-call | flops 125829120 | bytes 16777216 | tf_op jit(solution)/shard_map/advect/pallas_call | solution.py:574
  (7 shorter events, 0.1 us)
Async XLA Ops:
  0.6 17.9 %copy-start = (f32[250,12]{0,1:T(8,128)S(1)}, f32[250,12]{0,1:T(8,128)}, u32[]{:S(2)}) copy-start(f32[250,12]{0,1:T(8,128)} %param.12) | copy-start | bytes 36004
  0.6 18.1 %copy-start.1 = (f32[250]{0:T(256)S(1)}, f32[250]{0:T(256)}, u32[]{:S(2)}) copy-start(f32[250]{0:T(256)} %param.13) | copy-start | bytes 3004
  4.8 36.7 %all-to-all-start = ((bf16[32,128,128]{2,1,0:T(8,128)(2,1)}), bf16[32,128,128]{2,1,0:T(8,128)(2,1)S(1)}, u32[]{:S(2)}, u32[]{:S(2)}) async-start(bf16[32,128,128]{2,1,0:T(8,128)(2,1)} %regrid.1), calls=%async_computation | async-start | bytes 2097152 | tf_op jit(solution)/shard_map/all_to_all | solution.py:646
  15.2 12.0 %collective-permute-start.3 = (bf16[32,128]{1,0:T(8,128)(2,1)S(1)}, bf16[32,128]{1,0:T(8,128)(2,1)S(1)}, u32[]{:S(2)}, u32[]{:S(2)}) collective-permute-start(bf16[32,128]{1,0:T(8,128)(2,1)S(1)} %get-tuple-element.20), channel_id=1, source_target_pairs={{0,24},{8,0},{16,8},{24,16},{1,25},{9,1},{17,9},{25,17},{2,26},{10... | collective-permute-start | bytes 24584 | tf_op jit(solution)/shard_map/ppermute | solution.py:635
  16.8 10.4 %collective-permute-start.2 = (bf16[32,128]{1,0:T(8,128)(2,1)S(1)}, bf16[32,128]{1,0:T(8,128)(2,1)S(1)}, u32[]{:S(2)}, u32[]{:S(2)}) collective-permute-start(bf16[32,128]{1,0:T(8,128)(2,1)S(1)} %get-tuple-element.20), channel_id=1, source_target_pairs={{0,8},{8,16},{16,24},{24,0},{1,9},{9,17},{17,25},{25,1},{2,10},{10... | collective-permute-start | bytes 24584 | tf_op jit(solution)/shard_map/ppermute | solution.py:635
  16.8 22.3 %collective-permute-start.1 = (bf16[2,4,256,128]{3,2,1,0:T(8,128)(2,1)}, bf16[2,4,256,128]{3,2,1,0:T(8,128)(2,1)S(1)}, u32[]{:S(2)}, u32[]{:S(2)}) collective-permute-start(bf16[2,4,256,128]{3,2,1,0:T(8,128)(2,1)} %get-tuple-element.14), channel_id=1, source_target_pairs={{0,24},{8,0},{16,8},{24,16},{1,25},{9,1},{17,9},{25,17},{2,26},{10... | collective-permute-start | bytes 1572872 | tf_op jit(solution)/shard_map/ppermute | solution.py:635
  18.6 20.5 %collective-permute-start = (bf16[2,4,256,128]{3,2,1,0:T(8,128)(2,1)S(1)}, bf16[2,4,256,128]{3,2,1,0:T(8,128)(2,1)S(1)}, u32[]{:S(2)}, u32[]{:S(2)}) collective-permute-start(bf16[2,4,256,128]{3,2,1,0:T(8,128)(2,1)S(1)} %get-tuple-element.15), channel_id=1, source_target_pairs={{0,8},{8,16},{16,24},{24,0},{1,9},{9,17},{17,25},{25,1},{2,10},{10... | collective-permute-start | bytes 1572872 | tf_op jit(solution)/shard_map/ppermute | solution.py:635
  27.3 6.9 %collective-permute-start.5 = (bf16[320,128]{1,0:T(8,128)(2,1)S(1)}, bf16[320,128]{1,0:T(8,128)(2,1)S(1)}, u32[]{:S(2)}, u32[]{:S(2)}) collective-permute-start(bf16[320,128]{1,0:T(8,128)(2,1)S(1)} %get-tuple-element.26), channel_id=1, source_target_pairs={{0,7},{1,0},{2,1},{3,2},{4,3},{5,4},{6,5},{7,6},{8,15},{9,8},{10,9... | collective-permute-start | bytes 245768 | tf_op jit(solution)/shard_map/ppermute | solution.py:635
  31.6 7.5 %collective-permute-start.4 = (bf16[320,128]{1,0:T(8,128)(2,1)S(1)}, bf16[320,128]{1,0:T(8,128)(2,1)S(1)}, u32[]{:S(2)}, u32[]{:S(2)}) collective-permute-start(bf16[320,128]{1,0:T(8,128)(2,1)S(1)} %get-tuple-element.27), channel_id=1, source_target_pairs={{0,1},{1,2},{2,3},{3,4},{4,5},{5,6},{6,7},{7,0},{8,9},{9,10},{10,1... | collective-permute-start | bytes 245768 | tf_op jit(solution)/shard_map/ppermute | solution.py:635
